TPU v7x, 32 devices: a whole 2x2x4 slice. The times are simulated.
32 devices in a mesh: replica: 2 (over x), group: 8 (over z, y), tensor: 2 (over core).
Axes of the slice: x: 2, y: 2, z: 4, core: 2. Of those that a mesh axis runs over, the one named last changes fastest.
Arguments:
- hidden_in: bfloat16 [128, 128, 4096], P(('replica', 'group'), None, 'tensor'), parts along dimension 0, may hold values from -560 to 560
- norm_gain: float32 [4096], P('tensor'), may hold values from 0.5 to 8
- w_qkv: bfloat16 [1536, 4096], P('group', 'tensor'), may hold values from -0.09375 to 0.09375
- w_out: bfloat16 [1024, 4096], P(None, 'group'), may hold values from -0.1875 to 0.1875
- home_count: int32 [16], P('replica'), parts along dimension 0, may hold values from 1 to 8, 48 in all
- helper_start: int32 [2], P('replica'), parts along dimension 0, may hold values from 0 to 7
- segment_ids: int32 [128, 128], P('replica'), parts along dimension 0, may hold values from 0 to 2, never falling along the last dimension, each value on 1 to 64 neighbouring positions
Outputs:
- layer_out: bfloat16 [96, 128, 4096], P(('replica', 'group', 'tensor')), parts along dimension 0
- kv_cache: bfloat16 [128, 128, 512], P(('replica', 'group'), None, 'tensor'), parts along dimension 0
There are 2 independent parts, one for each index of `replica`. A program takes and returns all parts, laid end to end along the dimension named above; an argument that names none is the same for every part. Nothing has to cross between parts.
Inputs may be any that keep to these rules, and one draw needn't show every extreme that they name: `home_count`: the counts add up to 48; some home holds exactly 8 live blocks. `segment_ids`: never falling along a block's tokens.
All inputs are finite; a program needn't handle non-finite values.
Results may differ from a plain program's by a relative error of at most 0.012.
The roundings to bfloat16 on the way count: a program that leaves them out, or rounds other values in their place, can miss the bound.
Values may be sent and summed in bfloat16 or wider, within the bound.
A program may use at most 128 MiB of HBM per device.

v0:
```python
import jax
import jax.numpy as jnp
from jax import lax
from jax.sharding import PartitionSpec as P

HD = 128
Q_PER = 4


epsilon = 1e-05


def attend(projected, segments):
    block_len = projected.shape[1]
    queries = projected[:, :, :, :Q_PER]
    keys_part = projected[:, :, :, Q_PER]
    values_part = projected[:, :, :, Q_PER + 1]
    scores = jnp.einsum(
        "bihqd,bjhd->bhqij", queries, keys_part, preferred_element_type=jnp.float32
    ) * HD ** (-0.5)
    positions = jnp.arange(block_len)
    causal = positions[:, None] >= positions[None, :]
    allowed = causal[None] & (segments[:, :, None] == segments[:, None, :])
    scores = jnp.where(allowed[:, None, None], scores, -jnp.inf)
    highest = jnp.max(scores, axis=-1, keepdims=True)
    raised = jnp.exp(scores - highest)
    weights = (raised / jnp.sum(raised, axis=-1, keepdims=True)).astype(jnp.bfloat16)
    context = jnp.einsum(
        "bhqij,bjhd->bihqd", weights, values_part, preferred_element_type=jnp.float32
    )
    return context.astype(jnp.bfloat16).reshape(projected.shape[0] * block_len, -1)


def row_scale(floats, model_width):
    partial_sq = jnp.sum(floats * floats, axis=-1)
    summed = lax.psum(partial_sq, "tensor")
    return lax.rsqrt(summed / model_width + epsilon)


def per_device(hidden_in, norm_gain, w_qkv, w_out, home_count, helper_start, segment_ids):
    group_size = lax.axis_size("group")
    tensor_size = lax.axis_size("tensor")
    own_group = lax.axis_index("group")
    own_rank = lax.axis_index("tensor")
    slot_count, block_len, features = hidden_in.shape
    model_width = features * tensor_size
    capacity = min(8, group_size - 2)
    local_blocks = capacity // tensor_size
    half_rows = local_blocks * block_len
    first_helper = helper_start[0]
    ends = jnp.cumsum(home_count)
    begins = ends - home_count
    groups_iota = jnp.arange(group_size, dtype=jnp.int32)
    send_slot = (groups_iota - first_helper - begins[own_group]) % group_size
    send_live = send_slot < home_count[own_group]
    recv_slot = (own_group - first_helper - begins) % group_size
    recv_live = recv_slot < home_count
    placed = (begins + recv_slot) // group_size
    chosen = recv_live[None, :] & (
        placed[None, :] == jnp.arange(capacity, dtype=jnp.int32)[:, None]
    )
    source_of = jnp.sum(jnp.where(chosen, groups_iota[None, :], 0), axis=1)
    slot_of = jnp.sum(jnp.where(chosen, recv_slot[None, :], 0), axis=1)
    block_segments = jnp.take(segment_ids, source_of * slot_count + slot_of, axis=0)
    home_helper = (
        first_helper + begins[own_group] + jnp.arange(slot_count, dtype=jnp.int32)
    ) % group_size
    home_live = jnp.arange(slot_count, dtype=jnp.int32) < home_count[own_group]
    rows_full = lax.all_gather(w_qkv, "group", axis=0, tiled=True)
    contract = (((1,), (1,)), ((), ()))
    picked = jnp.take(hidden_in, jnp.minimum(send_slot, slot_count - 1), axis=0)
    outgoing = jnp.where(send_live[:, None, None], picked, jnp.zeros_like(picked))
    arrived = lax.all_to_all(outgoing, "group", split_axis=0, concat_axis=0, tiled=True)
    floats = jnp.take(arrived, source_of, axis=0).astype(jnp.float32)
    scale = row_scale(floats, model_width).reshape(-1)
    scaled = (floats * norm_gain).astype(jnp.bfloat16).reshape(capacity * block_len, features)
    summed = lax.psum_scatter(
        lax.dot_general(scaled, rows_full, contract, preferred_element_type=jnp.float32),
        "tensor",
        scatter_dimension=0,
        tiled=True,
    )
    own_scale = lax.dynamic_slice_in_dim(scale, own_rank * half_rows, half_rows, 0)
    projected = (summed * own_scale[:, None]).astype(jnp.bfloat16)
    projected = projected.reshape(local_blocks, block_len, -1, Q_PER + 2, HD)
    own_segments = lax.dynamic_slice_in_dim(
        block_segments, own_rank * local_blocks, local_blocks, 0
    )
    context = attend(projected, own_segments)
    mixed = jnp.dot(
        context,
        lax.all_gather(w_out, "group", axis=1, tiled=True),
        preferred_element_type=jnp.float32,
    )
    layer_out = mixed.astype(jnp.bfloat16).reshape(local_blocks, block_len, model_width)
    cache_local = projected[:, :, :, Q_PER:].reshape(local_blocks, block_len, -1)
    own_heads = lax.all_to_all(cache_local, "tensor", split_axis=2, concat_axis=0, tiled=True)
    returned = jnp.take(own_heads, jnp.minimum(placed, capacity - 1), axis=0)
    returned = jnp.where(recv_live[:, None, None], returned, jnp.zeros_like(returned))
    homeward = lax.all_to_all(returned, "group", split_axis=0, concat_axis=0, tiled=True)
    cache_rows = jnp.take(homeward, home_helper, axis=0)
    kv_cache = jnp.where(home_live[:, None, None], cache_rows, jnp.zeros_like(cache_rows))
    return (layer_out, kv_cache)


def solution(mesh):
    in_specs = (
        P(("replica", "group"), None, "tensor"),
        P("tensor"),
        P("group", "tensor"),
        P(None, "group"),
        P("replica"),
        P("replica"),
        P("replica", None),
    )
    out_specs = (
        P(("replica", "group", "tensor"), None, None),
        P(("replica", "group"), None, "tensor"),
    )
    return jax.shard_map(
        per_device, mesh=mesh, in_specs=in_specs, out_specs=out_specs, check_vma=False
    )
```

profile of v0, /device:TPU:9, one launch (start us, length us, event | category | flops | bytes accessed | tf_op | source)
XLA Modules:
  0.0 371.2 jit_solution(18044220888253475575)
XLA Ops:
  7.2 0.0 copy-start
  7.2 0.0 all-gather.3.cloned.1.call-start
  7.2 0.7 all-gather.3.cloned.1.call-update
  8.6 0.8 reduce-window.9
  9.4 1.3 dynamic_slice.15
  10.7 0.7 compare_and_fusion.1
  11.3 0.6 dynamic_slice.14
  11.9 0.6 fusion.17
  12.6 5.1 %gather_fusion = bf16[8,128,2048]{2,1,0:T(8,128)(2,1)} fusion(bf16[8,128,2048]{2,1,0:T(8,128)(2,1)} %param.7, s32[1024]{0:T(1024)S(1)} %pad_clamp_fusion.4), kind=kCustom, calls=%fused_computation | custom fusion | bytes 8388640 | tf_op jit(solution)/shard_map/jit(_take)/gather | solution.py:71
  17.7 1.3 compare_and_fusion.4
  18.9 5.2 %select_select_fusion = bf16[8,128,2048]{2,1,0:T(8,128)(2,1)} fusion(bf16[8,128,2048]{2,1,0:T(8,128)(2,1)} %gather_fusion, pred[8]{0:T(512)(128)(4,1)S(1)} %get-tuple-element.17, pred[8]{0:T(512)(128)(4,1)S(1)} %get-tuple-element.18), kind=kLoop, calls=%fused_computation.9 | loop fusion | flops 4194304 | bytes 8388624 | tf_op jit(solution)/shard_map/jit(_where)/select_n | solution.py:72
  24.1 0.0 copy-start.2
  24.1 5.8 %all-to-all-start = ((bf16[8,128,2048]{2,1,0:T(8,128)(2,1)}), bf16[8,128,2048]{2,1,0:T(8,128)(2,1)}, u32[]{:S(2)}, u32[]{:S(2)}) async-start(bf16[8,128,2048]{2,1,0:T(8,128)(2,1)} %select_select_fusion), calls=%async_computation | async-start | bytes 8388608 | tf_op jit(solution)/shard_map/all_to_all | solution.py:73
  29.9 0.0 reduce-scatter.2.cloned.1.call-start
  29.9 0.0 copy-done.2
  29.9 0.1 select_reduce_fusion
  30.1 0.1 broadcast_bitcast_fusion
  30.2 156.3 %all-to-all-done = bf16[8,128,2048]{2,1,0:T(8,128)(2,1)} async-done(((bf16[8,128,2048]{2,1,0:T(8,128)(2,1)}), bf16[8,128,2048]{2,1,0:T(8,128)(2,1)}, u32[]{:S(2)}, u32[]{:S(2)}) %all-to-all-start) | async-done | bytes 4194336 | tf_op jit(solution)/shard_map/all_to_all | solution.py:73
  186.4 2.9 gather_fusion.1
  189.4 0.0 copy-start.3
  189.4 2.2 bitcast_select_fusion
  191.6 0.0 all-gather.3.cloned.1.call-done
  191.6 0.0 copy-done.3
  191.6 9.6 %fusion.1 = f32[768,1536]{1,0:T(8,128)} fusion(bf16[1536,2048]{1,0:T(8,128)(2,1)} %all-gather.3.cloned.1.call-done, bf16[768,2048]{1,0:T(8,128)(2,1)} %bitcast_select_fusion, f32[2048]{0:T(1024)S(1)} %copy-done.3), kind=kOutput, calls=%fused_computation.10 | convolution fusion | flops 4836556800 | bytes 14163968 | tf_op jit(solution)/shard_map/dot_general | solution.py:78
  201.2 0.0 reduce-scatter.2.cloned.1.call-update
  201.2 0.0 all-gather.5.cloned.1.call-start
  201.3 0.7 all-gather.5.cloned.1.call-update
  202.6 0.0 copy-done
  202.6 0.6 gather_fusion.2
  203.2 0.6 compare_and_fusion.2
  203.8 0.1 broadcast_select_fusion
  204.0 0.1 compare_and_fusion
  204.1 1.0 multiply_reduce_fusion
  205.0 2.8 psum.7
  207.8 0.1 dynamic_slice.16
  207.9 8.8 %reduce-scatter.2.cloned.1.call-done = f32[384,1536]{1,0:T(8,128)} async-done(((f32[768,1536]{1,0:T(8,128)}), f32[384,1536]{1,0:T(8,128)}) %reduce-scatter.2.cloned.1.call-update) | async-done | bytes 2359312 | tf_op jit(solution)/shard_map/reduce_scatter | solution.py:77
  216.7 1.9 multiply_convert_fusion.2
  218.6 1.4 reshape.262
  220.0 0.0 copy-start.1
  220.0 0.4 slice.29
  220.4 0.7 fusion.26
  221.1 0.6 copy.45
  221.7 0.7 copy.44
  222.5 4.0 %all_to_all.28 = bf16[3,128,512]{1,0,2:T(4,128)(2,1)S(1)} all-to-all(bf16[3,128,512]{1,0,2:T(4,128)(2,1)S(1)} %bitcast.72), channel_id=1, replica_groups=mesh['replica'=2,'group'=8,'tensor'=2] {'tensor'}, dimensions={2} | all-to-all | bytes 786432 | tf_op jit(solution)/shard_map/all_to_all | solution.py:97
  226.5 0.0 copy-done.1
  226.5 0.1 copy.39
  226.5 0.0 slice-start
  226.5 0.2 copy.40
  226.7 0.6 gather_fusion.3
  227.3 0.9 select_select_fusion.2
  228.2 5.5 %all-to-all-start.2 = ((bf16[8,128,256]{2,1,0:T(8,128)(2,1)}), bf16[8,128,256]{2,1,0:T(8,128)(2,1)S(1)}, u32[]{:S(2)}, u32[]{:S(2)}) async-start(bf16[8,128,256]{2,1,0:T(8,128)(2,1)} %select_select_fusion.2), calls=%async_computation.3 | async-start | bytes 1048576 | tf_op jit(solution)/shard_map/all_to_all | solution.py:100
  233.7 0.0 slice-done
  233.7 1.8 fusion.27
  235.5 1.8 fusion.5
  237.3 0.7 copy.37
  238.0 0.6 reshape.263
  238.6 116.4 %all-gather.5.cloned.1.call-done = bf16[1024,4096]{1,0:T(8,128)(2,1)} async-done(((bf16[1024,512]{1,0:T(8,128)(2,1)}), bf16[1024,4096]{1,0:T(8,128)(2,1)}) %all-gather.5.cloned.1.call-update) | async-done | bytes 8388624 | tf_op jit(solution)/shard_map/all_gather | solution.py:92
  355.0 8.1 %convolution_convert_fusion = bf16[384,4096]{1,0:T(8,128)(2,1)} fusion(bf16[384,1024]{1,0:T(8,128)(2,1)S(1)} %reshape.263, bf16[1024,4096]{1,0:T(8,128)(2,1)} %all-gather.5.cloned.1.call-done), kind=kOutput, calls=%fused_computation.8 | convolution fusion | flops 3222798336 | bytes 12320768 | tf_op jit(solution)/shard_map/dot_general | solution.py:90
  363.1 0.0 all-to-all-done.2
  363.1 0.6 gather_fusion.4
  363.7 0.9 select_select_fusion.1
  (12 shorter events, 0.1 us)
Async XLA Ops:
  7.2 195.4 %copy-start = (s32[64,128]{1,0:T(8,128)S(1)}, s32[64,128]{1,0:T(8,128)}, u32[]{:S(2)}) copy-start(s32[64,128]{1,0:T(8,128)} %param.13) | copy-start | bytes 98308
  7.2 184.4 %all-gather.3.cloned.1.call-start = ((), (), s32[]{:S(2)}) async-start(), calls=%async_computation.4 | async-start | bytes 7077888 | tf_op jit(solution)/shard_map/all_gather | solution.py:69
  24.1 5.8 %copy-start.2 = (s32[8]{0:T(128)S(1)}, s32[8]{0:T(128)}, u32[]{:S(2)}) copy-start(s32[8]{0:T(128)} %param.11) | copy-start | bytes 100
  24.1 162.4 %all-to-all-start = ((bf16[8,128,2048]{2,1,0:T(8,128)(2,1)}), bf16[8,128,2048]{2,1,0:T(8,128)(2,1)}, u32[]{:S(2)}, u32[]{:S(2)}) async-start(bf16[8,128,2048]{2,1,0:T(8,128)(2,1)} %select_select_fusion), calls=%async_computation | async-start | bytes 8388608 | tf_op jit(solution)/shard_map/all_to_all | solution.py:73
  29.9 186.8 %reduce-scatter.2.cloned.1.call-start = ((), (), s32[]{:S(2)}) async-start(), calls=%async_computation.5 | async-start | bytes 7077888 | tf_op jit(solution)/shard_map/reduce_scatter | solution.py:77
  189.4 2.2 copy-start.3
  201.2 153.8 %all-gather.5.cloned.1.call-start = ((), (), s32[]{:S(2)}) async-start(), calls=%async_computation.6 | async-start | bytes 9437184 | tf_op jit(solution)/shard_map/all_gather | solution.py:92
  220.0 6.5 %copy-start.1 = (bf16[3,128,2,6,128]{4,3,2,1,0:T(8,128)(2,1)}, bf16[3,128,2,6,128]{4,3,2,1,0:T(8,128)(2,1)S(1)}, u32[]{:S(2)}) copy-start(bf16[3,128,2,6,128]{4,3,2,1,0:T(8,128)(2,1)S(1)} %reshape.262) | copy-start | bytes 3538948
  226.5 7.2 %slice-start = ((bf16[3,128,2,6,128]{4,3,2,1,0:T(8,128)(2,1)}), bf16[3,128,2,4,128]{4,3,2,1,0:T(4,128)(2,1)S(1)}, s32[]{:S(2)}) async-start(bf16[3,128,2,6,128]{4,3,2,1,0:T(8,128)(2,1)} %copy-done.1), calls=%async_computation.7 | async-start | bytes 1572864 | tf_op jit(solution)/shard_map/slice | solution.py:15
  228.2 134.9 %all-to-all-start.2 = ((bf16[8,128,256]{2,1,0:T(8,128)(2,1)}), bf16[8,128,256]{2,1,0:T(8,128)(2,1)S(1)}, u32[]{:S(2)}, u32[]{:S(2)}) async-start(bf16[8,128,256]{2,1,0:T(8,128)(2,1)} %select_select_fusion.2), calls=%async_computation.3 | async-start | bytes 1048576 | tf_op jit(solution)/shard_map/all_to_all | solution.py:100
Sparse Core Ops, SparseCore 0:
  10.2 172.9 all-gather.2
  201.3 15.3 reduce-scatter.1
  219.0 135.9 all-gather.4
where the time goes:
time: 376 us; the launch traced here: 371 us
  waiting for transfers between devices  283 us (75%)
  matrix products  21.3 us (6%)
  local copies, waits for them, and re-layouts  17.1 us (5%)
  other arithmetic  16.5 us (4%)
  between operations  15.3 us (4%)
  starting transfers between devices  11.4 us (3%)
  blocking collectives  6.8 us (2%)
    all_to_all x1, waiting for transfers between devices, per_device(): lax.all_to_all(outgoing, 'group', split_axis=0, concat_axis=0, tiled=True)  156 us
    all_gather x1, waiting for transfers between devices, per_device(): lax.all_gather(w_out, 'group', axis=1, tiled=True)  116 us
    dot_general x1, matrix products, per_device(): lax.dot_general(scaled, rows_full, contract, preferred_element_type=jnp.f...  9.6 us
    reduce_scatter x1, waiting for transfers between devices, per_device(): lax.psum_scatter(lax.dot_general(scaled, rows_full, contract, preferred_e...  8.8 us
    dot_general x1, matrix products, per_device(): jnp.dot(context, lax.all_gather(w_out, 'group', axis=1, tiled=True), pref...  8.15 us
  transfers between devices with their start and end apart: 5, of which 3 were waited for; matrix products, arithmetic and copies ran while one was open for 12% of the time, Pallas kernels for 0%

commit v1 on v0

v1 whole, which is shorter than its diff:
```python
import jax
import jax.numpy as jnp
from jax import lax
from jax.sharding import PartitionSpec as P

HD = 128
Q_PER = 4


epsilon = 1e-05


def attend(projected, segments):
    block_len = projected.shape[1]
    queries = projected[:, :, :, :Q_PER]
    keys_part = projected[:, :, :, Q_PER]
    values_part = projected[:, :, :, Q_PER + 1]
    scores = jnp.einsum(
        "bihqd,bjhd->bhqij", queries, keys_part, preferred_element_type=jnp.float32
    ) * HD ** (-0.5)
    positions = jnp.arange(block_len)
    causal = positions[:, None] >= positions[None, :]
    allowed = causal[None] & (segments[:, :, None] == segments[:, None, :])
    scores = jnp.where(allowed[:, None, None], scores, -jnp.inf)
    highest = jnp.max(scores, axis=-1, keepdims=True)
    raised = jnp.exp(scores - highest)
    weights = (raised / jnp.sum(raised, axis=-1, keepdims=True)).astype(jnp.bfloat16)
    context = jnp.einsum(
        "bhqij,bjhd->bihqd", weights, values_part, preferred_element_type=jnp.float32
    )
    return context.astype(jnp.bfloat16).reshape(projected.shape[0] * block_len, -1)


def row_scale(floats, model_width):
    partial_sq = jnp.sum(floats * floats, axis=-1)
    summed = lax.psum(partial_sq, "tensor")
    return lax.rsqrt(summed / model_width + epsilon)


def project_and_attend(hidden_in, norm_gain, rows_full, segments, tensor_size):
    slot_count, block_len, features = hidden_in.shape
    floats = hidden_in.astype(jnp.float32)
    scale = row_scale(floats, features * tensor_size).reshape(-1)
    scaled = (floats * norm_gain).astype(jnp.bfloat16).reshape(-1, features)
    contract = (((1,), (1,)), ((), ()))
    partial = lax.dot_general(
        scaled, rows_full, contract, preferred_element_type=jnp.float32
    )
    summed = lax.psum_scatter(partial, "tensor", scatter_dimension=1, tiled=True)
    projected = (summed * scale[:, None]).astype(jnp.bfloat16)
    projected = projected.reshape(slot_count, block_len, -1, Q_PER + 2, HD)
    context = attend(projected, segments).reshape(slot_count, block_len, -1)
    cache = projected[:, :, :, Q_PER:].reshape(slot_count, block_len, -1)
    return context, cache


def per_device(hidden_in, norm_gain, w_qkv, w_out, home_count, helper_start, segment_ids):
    group_size = lax.axis_size("group")
    tensor_size = lax.axis_size("tensor")
    own_group = lax.axis_index("group")
    own_rank = lax.axis_index("tensor")
    slot_count, block_len, features = hidden_in.shape
    capacity = min(8, group_size - 2)
    local_blocks = capacity // tensor_size
    first_helper = helper_start[0]
    ends = jnp.cumsum(home_count)
    begins = ends - home_count
    groups_iota = jnp.arange(group_size, dtype=jnp.int32)
    send_slot = (groups_iota - first_helper - begins[own_group]) % group_size
    recv_slot = (own_group - first_helper - begins) % group_size
    recv_live = recv_slot < home_count
    placed = (begins + recv_slot) // group_size
    chosen = recv_live[None, :] & (
        placed[None, :] == jnp.arange(capacity, dtype=jnp.int32)[:, None]
    )
    source_of = jnp.sum(jnp.where(chosen, groups_iota[None, :], 0), axis=1)
    home_live = jnp.arange(slot_count, dtype=jnp.int32) < home_count[own_group]
    segments = lax.dynamic_slice_in_dim(segment_ids, own_group * slot_count, slot_count, 0)
    rows_full = lax.all_gather(w_qkv, "group", axis=0, tiled=True)
    part_rows = w_out.shape[0] // tensor_size
    own_part = lax.dynamic_slice_in_dim(w_out, own_rank * part_rows, part_rows, 0)
    out_part = lax.all_gather(own_part, "group", axis=1, tiled=True)
    out_full = lax.all_gather(out_part, "tensor", axis=0, tiled=True)
    context, cache = project_and_attend(
        hidden_in, norm_gain, rows_full, segments, tensor_size
    )
    kv_cache = jnp.where(home_live[:, None, None], cache, jnp.zeros_like(cache))
    outgoing = jnp.take(context, jnp.minimum(send_slot, slot_count - 1), axis=0)
    arrived = lax.all_to_all(outgoing, "group", split_axis=0, concat_axis=0, tiled=True)
    helped = jnp.take(arrived, source_of, axis=0)
    rows = lax.all_to_all(helped, "tensor", split_axis=0, concat_axis=2, tiled=True)
    mixed = jnp.dot(
        rows.reshape(local_blocks * block_len, -1),
        out_full,
        preferred_element_type=jnp.float32,
    )
    layer_out = mixed.astype(jnp.bfloat16).reshape(local_blocks, block_len, -1)
    return (layer_out, kv_cache)


def solution(mesh):
    in_specs = (
        P(("replica", "group"), None, "tensor"),
        P("tensor"),
        P("group", "tensor"),
        P(None, "group"),
        P("replica"),
        P("replica"),
        P("replica", None),
    )
    out_specs = (
        P(("replica", "group", "tensor"), None, None),
        P(("replica", "group"), None, "tensor"),
    )
    return jax.shard_map(
        per_device, mesh=mesh, in_specs=in_specs, out_specs=out_specs, check_vma=False
    )
```

time: 376 us -> 278 us (0.74)
  waiting for transfers between devices: 283 us -> 190 us
  starting transfers between devices: 11.4 us -> 5.65 us
    all_to_all x1, waiting for transfers between devices: 156 us -> 20.9 us  [per_device(): lax.all_to_all(outgoing, 'group', split_axis=0, concat_axis=0, tiled=True)]
    all_gather x1, waiting for transfers between devices: 0.01 us -> 93.4 us  [per_device(): rows_full = lax.all_gather(w_qkv, 'group', axis=0, tiled=True)]
    all_gather x1 -> x2, waiting for transfers between devices: 116 us -> 64 us  [the longest x1 64 us: per_device(): out_part = lax.all_gather(own_part, 'group', axis=1, tiled=True)]
    select_n x8 -> x6, other arithmetic: 9.95 us -> 4.07 us  [the longest x2 3.01 us: per_device(): outgoing = jnp.take(context, jnp.minimum(send_slot, slot_count - 1), axis=0)]
    all_to_all x1 -> x0, starting transfers between devices: 5.49 us -> none  [per_device(): lax.all_to_all(returned, 'group', split_axis=0, concat_axis=0, tiled=True)]
    gather x5 -> x2, local copies, waits for them, and re-layouts: 9.71 us -> 4.68 us  [the longest x1 2.86 us: per_device(): outgoing = jnp.take(context, jnp.minimum(send_slot, slot_count - 1), axis=0)]
    unnamed x9 -> x14, local copies, waits for them, and re-layouts: 0.62 us -> 5.12 us
    reduce_sum x1, other arithmetic: 0.95 us -> 5.42 us  [row_scale(): partial_sq = jnp.sum(floats * floats, axis=-1)]
  transfers between devices with their start and end apart: 5 -> 5, of which waited for: 3 -> 4; matrix products, arithmetic and copies ran while one was open for 12% -> 17% of each run, Pallas kernels for 0% -> 0%
where the time goes in v1:
time: 278 us; the launch traced here: 275 us
  waiting for transfers between devices  190 us (68%)
  matrix products  23.4 us (8%)
  local copies, waits for them, and re-layouts  18.8 us (7%)
  between operations  14.6 us (5%)
  other arithmetic  14.5 us (5%)
  blocking collectives  8.23 us (3%)
  starting transfers between devices  5.65 us (2%)
    all_gather x1, waiting for transfers between devices, per_device(): rows_full = lax.all_gather(w_qkv, 'group', axis=0, tiled=True)  93.4 us
    all_gather x1, waiting for transfers between devices, per_device(): out_part = lax.all_gather(own_part, 'group', axis=1, tiled=True)  64 us
    all_to_all x1, waiting for transfers between devices, per_device(): lax.all_to_all(outgoing, 'group', split_axis=0, concat_axis=0, tiled=True)  20.9 us
    dot_general x1, matrix products, project_and_attend(): lax.dot_general(scaled, rows_full, contract, preferred_element_type=jnp.f...  11.8 us
    reduce_scatter x1, waiting for transfers between devices, project_and_attend(): lax.psum_scatter(partial, 'tensor', scatter_dimension=1, tiled=True)  10.5 us
    dot_general x1, matrix products, per_device(): jnp.dot(rows.reshape(local_blocks * block_len, -1), out_full, preferred_e...  8.17 us
  transfers between devices with their start and end apart: 5, of which 4 were waited for; matrix products, arithmetic and copies ran while one was open for 17% of the time, Pallas kernels for 0%

profile of v1, /device:TPU:9, one launch (start us, length us, event | category | flops | bytes accessed | tf_op | source)
XLA Modules:
  0.0 274.7 jit_solution(15764235409492841842)
XLA Ops:
  7.2 0.0 copy-start
  7.2 0.0 all-gather.4.cloned.1.call-start
  7.2 0.7 all-gather.4.cloned.1.call-update
  7.9 0.0 all-gather.6.cloned.1.call-start
  8.0 0.4 copy-done
  8.4 0.8 constant_dynamic-slice_fusion.1
  9.2 0.0 all-gather.6.cloned.1.call-update
  9.2 0.0 reduce-scatter.2.cloned.1.call-start
  9.3 5.4 %fusion.1 = (f32[8,128]{1,0:T(8,128)S(1)}, bf16[8,128,2048]{2,1,0:T(8,128)(2,1)}) fusion(bf16[8,128,2048]{2,1,0:T(8,128)(2,1)} %param.7, f32[2048]{0:T(1024)} %param.8), kind=kLoop, calls=%fused_computation.5 | loop fusion | flops 10484736 | bytes 8400896 | tf_op jit(solution)/shard_map/reduce_sum | solution.py:35
  14.7 93.4 %all-gather.4.cloned.1.call-done = bf16[1536,2048]{1,0:T(8,128)(2,1)} async-done(((bf16[192,2048]{1,0:T(8,128)(2,1)}), bf16[1536,2048]{1,0:T(8,128)(2,1)}) %all-gather.4.cloned.1.call-update) | async-done | bytes 6291472 | tf_op jit(solution)/shard_map/all_gather | solution.py:79
  108.1 11.8 %fusion.17 = f32[1024,1536]{1,0:T(8,128)} fusion(bf16[1024,2048]{1,0:T(8,128)(2,1)} %bitcast.73, bf16[1536,2048]{1,0:T(8,128)(2,1)} %all-gather.4.cloned.1.call-done), kind=kOutput, calls=%fused_computation.61 | convolution fusion | flops 6442450944 | bytes 16777216 | tf_op jit(solution)/shard_map/dot_general | solution.py:46
  119.9 0.0 reduce-scatter.2.cloned.1.call-update
  119.9 0.0 copy-start.1
  119.9 0.0 all-gather.8.cloned.1.call-start
  120.0 64.0 %all-gather.6.cloned.1.call-done = bf16[512,4096]{1,0:T(8,128)(2,1)} async-done(((bf16[512,512]{1,0:T(8,128)(2,1)}), bf16[512,4096]{1,0:T(8,128)(2,1)}) %all-gather.6.cloned.1.call-update) | async-done | bytes 4194320 | tf_op jit(solution)/shard_map/all_gather | solution.py:82
  184.0 0.0 all-gather.8.cloned.1.call-update
  184.7 0.0 copy-done.1
  184.7 0.2 reduce-window.9
  184.9 0.6 fusion.14
  185.5 0.0 copy-start.3
  185.5 0.6 dynamic_slice.12
  186.1 0.0 copy-done.3
  186.1 3.2 %psum.7 = f32[8,128]{1,0:T(8,128)S(1)} all-reduce(f32[8,128]{1,0:T(8,128)S(1)} %get-tuple-element.5), channel_id=1, replica_groups=mesh['replica'=2,'group'=8,'tensor'=2] {'tensor'}, use_global_device_ids=true, to_apply=%region_4.5 | all-reduce | flops 1024 | bytes 8192 | tf_op jit(solution)/shard_map/psum | solution.py:36
  189.3 0.7 fusion.12
  189.9 0.7 compare_and_fusion.1
  190.6 0.7 constant_dynamic-slice_fusion
  191.3 0.2 compare_and_fusion
  191.5 10.5 %reduce-scatter.2.cloned.1.call-done = f32[1024,768]{1,0:T(8,128)} async-done(((f32[1024,1536]{1,0:T(8,128)}), f32[1024,768]{1,0:T(8,128)}) %reduce-scatter.2.cloned.1.call-update) | async-done | bytes 3145744 | tf_op jit(solution)/shard_map/reduce_scatter | solution.py:49
  202.0 2.1 multiply_convert_fusion
  204.1 1.6 copy.41
  205.8 1.8 copy.55
  207.6 1.0 slice.22
  208.7 2.5 copy.54
  211.2 0.2 copy.53
  211.4 1.8 fusion.16
  213.3 0.4 fusion.2
  213.7 1.6 convolution_convert_fusion.1
  215.3 2.4 copy.46
  217.7 0.0 copy-start.2
  217.7 0.0 copy-start.4
  217.7 2.9 %gather_fusion = bf16[8,128,512]{2,1,0:T(8,128)(2,1)} fusion(bf16[8,128,512]{2,1,0:T(8,128)(2,1)} %copy.46, s32[1024]{0:T(1024)S(1)} %pad_clamp_fusion.1), kind=kCustom, calls=%fused_computation | custom fusion | bytes 2097184 | tf_op jit(solution)/shard_map/jit(_take)/gather | solution.py:88
  220.5 2.4 broadcast_select_fusion
  222.9 5.5 %all-to-all-start = ((bf16[8,128,512]{2,1,0:T(8,128)(2,1)}), bf16[8,128,512]{2,1,0:T(8,128)(2,1)}, u32[]{:S(2)}, u32[]{:S(2)}) async-start(bf16[8,128,512]{2,1,0:T(8,128)(2,1)} %broadcast_select_fusion), calls=%async_computation.1 | async-start | bytes 2097152 | tf_op jit(solution)/shard_map/all_to_all | solution.py:89
  228.4 0.6 dynamic_slice.15
  229.0 0.6 iota_compare_fusion.2
  229.6 0.0 copy-done.2
  229.6 0.0 copy-done.4
  229.7 0.1 select_reduce_fusion
  229.9 0.3 copy.48
  230.2 0.9 broadcast_select_fusion.2
  231.1 20.9 %all-to-all-done = bf16[8,128,512]{2,1,0:T(8,128)(2,1)} async-done(((bf16[8,128,512]{2,1,0:T(8,128)(2,1)}), bf16[8,128,512]{2,1,0:T(8,128)(2,1)}, u32[]{:S(2)}, u32[]{:S(2)}) %all-to-all-start) | async-done | bytes 1048608 | tf_op jit(solution)/shard_map/all_to_all | solution.py:89
  252.0 1.8 gather_fusion.1
  253.8 0.1 broadcast_select_fusion.1
  254.0 5.1 %all_to_all.20 = bf16[6,128,512]{2,1,0:T(8,128)(2,1)S(1)} all-to-all(bf16[6,128,512]{2,1,0:T(8,128)(2,1)S(1)} %broadcast_select_fusion.1), channel_id=1, replica_groups=mesh['replica'=2,'group'=8,'tensor'=2] {'tensor'}, dimensions={0} | all-to-all | bytes 1572864 | tf_op jit(solution)/shard_map/all_to_all | solution.py:91
  259.0 0.8 copy.47
  259.8 0.1 copy.56
  260.0 0.0 all-gather.8.cloned.1.call-done
  260.0 8.2 %convolution_convert_fusion = bf16[384,4096]{1,0:T(8,128)(2,1)} fusion(bf16[384,1024]{1,0:T(8,128)(2,1)S(1)} %bitcast.78, bf16[1024,4096]{1,0:T(8,128)(2,1)} %all-gather.8.cloned.1.call-done), kind=kOutput, calls=%fused_computation.6 | convolution fusion | flops 3222798336 | bytes 12320768 | tf_op jit(solution)/shard_map/dot_general | solution.py:92
  (9 shorter events, 0.1 us)
Async XLA Ops:
  7.2 1.2 copy-start
  7.2 100.9 %all-gather.4.cloned.1.call-start = ((), (), s32[]{:S(2)}) async-start(), calls=%async_computation.3 | async-start | bytes 7077888 | tf_op jit(solution)/shard_map/all_gather | solution.py:79
  7.9 176.1 %all-gather.6.cloned.1.call-start = ((), (), s32[]{:S(2)}) async-start(), calls=%async_computation.5 | async-start | bytes 4718592 | tf_op jit(solution)/shard_map/all_gather | solution.py:82
  9.2 192.8 %reduce-scatter.2.cloned.1.call-start = ((), (), s32[]{:S(2)}) async-start(), calls=%async_computation.4 | async-start | bytes 9437184 | tf_op jit(solution)/shard_map/reduce_scatter | solution.py:49
  119.9 64.8 %copy-start.1 = (s32[8]{0:T(128)S(1)}, s32[8]{0:T(128)}, u32[]{:S(2)}) copy-start(s32[8]{0:T(128)} %param.11) | copy-start | bytes 100
  119.9 140.0 %all-gather.8.cloned.1.call-start = ((), (), s32[]{:S(2)}) async-start(), calls=%async_computation.6 | async-start | bytes 12582912 | tf_op jit(solution)/shard_map/all_gather | solution.py:83
  185.5 0.6 copy-start.3
  217.7 12.0 %copy-start.2 = (s32[8]{0:T(128)S(1)}, s32[8]{0:T(128)}, u32[]{:S(2)}) copy-start(s32[8]{0:T(128)} %get-tuple-element.3) | copy-start | bytes 100
  217.7 12.0 %copy-start.4 = (s32[8]{0:T(128)S(1)}, s32[8]{0:T(128)}, u32[]{:S(2)}) copy-start(s32[8]{0:T(128)} %copy-done.3) | copy-start | bytes 100
  222.9 29.1 %all-to-all-start = ((bf16[8,128,512]{2,1,0:T(8,128)(2,1)}), bf16[8,128,512]{2,1,0:T(8,128)(2,1)}, u32[]{:S(2)}, u32[]{:S(2)}) async-start(bf16[8,128,512]{2,1,0:T(8,128)(2,1)} %broadcast_select_fusion), calls=%async_computation.1 | async-start | bytes 2097152 | tf_op jit(solution)/shard_map/all_to_all | solution.py:89
Sparse Core Ops, SparseCore 0:
  10.2 97.8 all-gather.3
  110.7 73.2 all-gather.5
  186.3 15.6 reduce-scatter.1
  203.5 21.0 all-gather.7

commit v2 on v1

--- a/solution.py
+++ b/solution.py
@@ -1,6 +1,9 @@
+import functools
 import jax
 import jax.numpy as jnp
 from jax import lax
+from jax.experimental import pallas as pl
+from jax.experimental.pallas import tpu as pltpu
 from jax.sharding import PartitionSpec as P
 
 HD = 128
@@ -35,6 +38,102 @@
     partial_sq = jnp.sum(floats * floats, axis=-1)
     summed = lax.psum(partial_sq, "tensor")
     return lax.rsqrt(summed / model_width + epsilon)
+
+
+def gather_kernel(line, shard_ref, full_ref, own_sem, send_sem, recv_sem):
+    pool = lax.axis_index("replica")
+    group = lax.axis_index("group")
+    core = lax.axis_index("tensor")
+    z, y = group // 2, group % 2
+    rows = shard_ref.shape[0]
+    half, quarter = rows // 2, rows // 4
+    mine = pl.ds(pool * half, half)
+    across = (1 - pool, group, core)
+    beside = (pool, z * 2 + (1 - y), core)
+
+    def along(step):
+        return (z + step) % line
+
+    barrier = pltpu.get_barrier_semaphore()
+    peers = [(pool, along(d) * 2 + y, core) for d in range(1, line)] + [across, beside]
+    for peer in peers:
+        pl.semaphore_signal(barrier, inc=1, device_id=peer, device_id_type=pl.DeviceIdType.MESH)
+    pl.semaphore_wait(barrier, len(peers))
+
+    def remote(index, src, dst, peer):
+        return pltpu.make_async_remote_copy(
+            src_ref=src,
+            dst_ref=dst,
+            send_sem=send_sem.at[index],
+            recv_sem=recv_sem.at[index],
+            device_id=peer,
+            device_id_type=pl.DeviceIdType.MESH,
+        )
+
+    def passed(index, source, begin, count, peer):
+        place = full_ref.at[source, pl.ds(begin, count)]
+        return remote(index, place, place, peer)
+
+    own = pltpu.make_async_copy(shard_ref, full_ref.at[group], own_sem)
+    own.start()
+    first = [
+        remote(d - 1, shard_ref.at[mine], full_ref.at[group, mine], (pool, along(d) * 2 + y, core))
+        for d in range(1, line)
+    ]
+    for copy in first:
+        copy.start()
+    sideways = [remote(line - 1, shard_ref.at[mine], full_ref.at[group, mine], beside)]
+    sideways[0].start()
+    over, second, third = [], [], []
+    for d in range(1, line):
+        first[d - 1].wait_recv()
+        source = along(line - d) * 2 + y
+        over.append(passed(line + d - 1, source, pool * half, half, across))
+        over[-1].start()
+        sideways.append(passed(2 * line + d - 2, source, pool * half, half, beside))
+        sideways[-1].start()
+    base = 3 * line - 2
+    for d in range(line):
+        sideways[d].wait_recv()
+        source = along(line - d) * 2 + (1 - y)
+        begin, count = (0, half) if d == 0 else (quarter, quarter)
+        second.append(passed(base + d, source, pool * half + begin, count, across))
+        second[-1].start()
+        if d > 0:
+            over[d - 1].wait_recv()
+            source = along(line - d) * 2 + y
+            third.append(
+                passed(base + line + d - 1, source, (1 - pool) * half, quarter, beside)
+            )
+            third[-1].start()
+    for copy in second + third:
+        copy.wait_recv()
+    for copy in first + sideways + over + second + third:
+        copy.wait_send()
+    own.wait()
+
+
+def gather_rows(shard, group_size, collective_id):
+    line = group_size // 2
+    copies = 5 * line - 3
+    full = pl.pallas_call(
+        functools.partial(gather_kernel, line),
+        out_shape=jax.ShapeDtypeStruct((group_size,) + shard.shape, shard.dtype),
+        in_specs=[pl.BlockSpec(memory_space=pl.ANY)],
+        out_specs=pl.BlockSpec(memory_space=pl.ANY),
+        scratch_shapes=[
+            pltpu.SemaphoreType.DMA,
+            pltpu.SemaphoreType.DMA((copies,)),
+            pltpu.SemaphoreType.DMA((copies,)),
+        ],
+        compiler_params=pltpu.CompilerParams(
+            collective_id=collective_id, has_side_effects=True
+        ),
+        cost_estimate=pl.CostEstimate(
+            flops=0, bytes_accessed=200_000_000, transcendentals=0
+        ),
+    )(shard)
+    return full.reshape((-1,) + shard.shape[1:])
 
 
 def project_and_attend(hidden_in, norm_gain, rows_full, segments, tensor_size):
@@ -76,7 +175,10 @@
     source_of = jnp.sum(jnp.where(chosen, groups_iota[None, :], 0), axis=1)
     home_live = jnp.arange(slot_count, dtype=jnp.int32) < home_count[own_group]
     segments = lax.dynamic_slice_in_dim(segment_ids, own_group * slot_count, slot_count, 0)
-    rows_full = lax.all_gather(w_qkv, "group", axis=0, tiled=True)
+    if (lax.axis_size("replica"), group_size) == (2, 8):
+        rows_full = gather_rows(w_qkv, group_size, 0)
+    else:
+        rows_full = lax.all_gather(w_qkv, "group", axis=0, tiled=True)
     part_rows = w_out.shape[0] // tensor_size
     own_part = lax.dynamic_slice_in_dim(w_out, own_rank * part_rows, part_rows, 0)
     out_part = lax.all_gather(own_part, "group", axis=1, tiled=True)

time: 278 us -> 223 us (0.80)
  waiting for transfers between devices: 190 us -> 53.2 us
  Pallas kernels: 0 us -> 82.4 us
  matrix products: 23.4 us -> 20.3 us
    all_gather x1 -> x0, waiting for transfers between devices: 93.4 us -> none  [per_device(): rows_full = lax.all_gather(w_qkv, 'group', axis=0, tiled=True)]
    pallas_call x0 -> x1, Pallas kernels: none -> 82.4 us  [gather_rows(): pl.pallas_call(functools.partial(gather_kernel, line), out_shape=jax.Shap...]
    all_gather x1, waiting for transfers between devices: 64 us -> 19.8 us  [per_device(): out_part = lax.all_gather(own_part, 'group', axis=1, tiled=True)]
    dot_general x1, matrix products: 11.8 us -> 8.67 us  [project_and_attend(): lax.dot_general(scaled, rows_full, contract, preferred_element_type=jnp.f...]
    unnamed x14 -> x18, local copies, waits for them, and re-layouts: 5.12 us -> 6.22 us
  transfers between devices with their start and end apart: 5 -> 4, of which waited for: 4 -> 3; matrix products, arithmetic and copies ran while one was open for 17% -> 19% of each run, Pallas kernels for 0% -> 38%
where the time goes in v2:
time: 223 us; the launch traced here: 219 us
  Pallas kernels  82.4 us (37%)
  waiting for transfers between devices  53.2 us (24%)
  matrix products  20.3 us (9%)
  local copies, waits for them, and re-layouts  19.9 us (9%)
  between operations  16.4 us (7%)
  other arithmetic  12.6 us (6%)
  blocking collectives  8.52 us (4%)
  starting transfers between devices  5.61 us (3%)
    pallas_call x1, Pallas kernels, gather_rows(): pl.pallas_call(functools.partial(gather_kernel, line), out_shape=jax.Shap...  82.4 us
    all_to_all x1, waiting for transfers between devices, per_device(): lax.all_to_all(outgoing, 'group', split_axis=0, concat_axis=0, tiled=True)  20.8 us
    all_gather x1, waiting for transfers between devices, per_device(): out_part = lax.all_gather(own_part, 'group', axis=1, tiled=True)  19.8 us
    reduce_scatter x1, waiting for transfers between devices, project_and_attend(): lax.psum_scatter(partial, 'tensor', scatter_dimension=1, tiled=True)  12.6 us
    dot_general x1, matrix products, project_and_attend(): lax.dot_general(scaled, rows_full, contract, preferred_element_type=jnp.f...  8.67 us
    dot_general x1, matrix products, per_device(): jnp.dot(rows.reshape(local_blocks * block_len, -1), out_full, preferred_e...  8.16 us
    unnamed x18, local copies, waits for them, and re-layouts  6.22 us
    all_to_all x1, starting transfers between devices, per_device(): lax.all_to_all(outgoing, 'group', split_axis=0, concat_axis=0, tiled=True)  5.49 us
  transfers between devices with their start and end apart: 4, of which 3 were waited for; matrix products, arithmetic and copies ran while one was open for 19% of the time, Pallas kernels for 38%

profile of v2, /device:TPU:9, one launch (start us, length us, event | category | flops | bytes accessed | tf_op | source)
XLA Modules:
  0.0 218.9 jit_solution(15022842081956272111)
XLA Ops:
  8.0 0.0 copy-start
  8.0 0.0 all-gather.3.cloned.1.call-start
  8.1 1.2 copy-done
  9.2 0.8 constant_dynamic-slice_fusion.1
  10.1 0.0 all-gather.3.cloned.1.call-update
  10.1 0.0 copy-start.2
  10.1 0.0 reduce-scatter.2.cloned.1.call-start
  10.1 82.4 %shard_map.86 = bf16[8,192,2048]{2,1,0:T(8,128)(2,1)} custom-call(bf16[192,2048]{1,0:T(8,128)(2,1)} %shard_ref.1), custom_call_target="tpu_custom_call" | custom-call | bytes 200000000 | tf_op jit(solution)/shard_map/pallas_call | solution.py:119
  92.5 0.0 copy-done.2
  92.5 0.0 copy-start.1
  92.5 3.7 %fusion.1 = (f32[8,128]{1,0:T(8,128)S(1)}, bf16[8,128,2048]{2,1,0:T(8,128)(2,1)S(1)}) fusion(bf16[8,128,2048]{2,1,0:T(8,128)(2,1)} %param.7, f32[2048]{0:T(1024)S(1)} %copy-done.2), kind=kLoop, calls=%fused_computation.5 | loop fusion | flops 10484736 | bytes 8400896 | tf_op jit(solution)/shard_map/reduce_sum | solution.py:38
  96.2 0.4 copy-done.1
  96.6 8.7 %fusion.17 = f32[1024,1536]{1,0:T(8,128)} fusion(bf16[1024,2048]{1,0:T(8,128)(2,1)S(1)} %bitcast.75, bf16[1536,2048]{1,0:T(8,128)(2,1)S(1)} %bitcast.73), kind=kOutput, calls=%fused_computation.61 | convolution fusion | flops 6442450944 | bytes 16777216 | tf_op jit(solution)/shard_map/dot_general | solution.py:145
  105.2 0.0 reduce-scatter.2.cloned.1.call-update
  105.3 0.0 copy-start.3
  105.3 0.0 all-gather.5.cloned.1.call-start
  105.3 19.8 %all-gather.3.cloned.1.call-done = bf16[512,4096]{1,0:T(8,128)(2,1)} async-done(((bf16[512,512]{1,0:T(8,128)(2,1)}), bf16[512,4096]{1,0:T(8,128)(2,1)}) %all-gather.3.cloned.1.call-update) | async-done | bytes 4194320 | tf_op jit(solution)/shard_map/all_gather | solution.py:184
  125.1 0.0 all-gather.5.cloned.1.call-update
  125.8 0.0 copy-done.3
  125.8 0.2 reduce-window.9
  126.0 0.5 fusion.14
  126.5 0.0 copy-start.5
  126.5 0.6 dynamic_slice.12
  127.1 0.0 copy-done.5
  127.1 3.3 %psum.7 = f32[8,128]{1,0:T(8,128)S(1)} all-reduce(f32[8,128]{1,0:T(8,128)S(1)} %get-tuple-element.5), channel_id=1, replica_groups=mesh['replica'=2,'group'=8,'tensor'=2] {'tensor'}, use_global_device_ids=true, to_apply=%region_4.5 | all-reduce | flops 1024 | bytes 8192 | tf_op jit(solution)/shard_map/psum | solution.py:39
  130.4 0.7 fusion.12
  131.0 0.7 compare_and_fusion.1
  131.7 0.7 constant_dynamic-slice_fusion
  132.4 0.2 compare_and_fusion
  132.6 12.6 %reduce-scatter.2.cloned.1.call-done = f32[1024,768]{1,0:T(8,128)} async-done(((f32[1024,1536]{1,0:T(8,128)}), f32[1024,768]{1,0:T(8,128)}) %reduce-scatter.2.cloned.1.call-update) | async-done | bytes 3145744 | tf_op jit(solution)/shard_map/reduce_scatter | solution.py:148
  145.2 2.1 multiply_convert_fusion
  147.4 1.6 copy.41
  149.0 1.8 copy.55
  150.8 1.0 slice.22
  151.9 2.4 %copy.54 = bf16[8,128,1,4,128]{4,1,3,0,2:T(8,128)(2,1)} copy(bf16[8,128,1,4,128]{1,0,4,3,2:T(8,128)(2,1)} %slice.22) | data formatting | bytes 2097152
  154.4 0.2 copy.53
  154.6 1.9 fusion.16
  156.5 0.4 fusion.2
  156.9 1.6 convolution_convert_fusion.1
  158.5 2.4 %copy.46 = bf16[8,128,512]{2,1,0:T(8,128)(2,1)} copy(bf16[8,128,512]{1,2,0:T(8,128)(2,1)} %bitcast.79) | data formatting | bytes 2097152 | tf_op jit(solution)/shard_map/reshape;reshape | solution.py:151
  160.9 0.0 copy-start.4
  160.9 0.0 copy-start.6
  160.9 2.9 %gather_fusion = bf16[8,128,512]{2,1,0:T(8,128)(2,1)} fusion(bf16[8,128,512]{2,1,0:T(8,128)(2,1)} %copy.46, s32[1024]{0:T(1024)S(1)} %pad_clamp_fusion.1), kind=kCustom, calls=%fused_computation | custom fusion | bytes 2097184 | tf_op jit(solution)/shard_map/jit(_take)/gather | solution.py:190
  163.7 2.4 %broadcast_select_fusion = bf16[8,128,512]{2,1,0:T(8,128)(2,1)} fusion(bf16[8,128,512]{2,1,0:T(8,128)(2,1)} %gather_fusion, pred[8]{0:T(512)(128)(4,1)S(1)} %compare_and_fusion.1), kind=kLoop, calls=%fused_computation.15 | loop fusion | flops 524288 | bytes 2097160 | tf_op jit(solution)/shard_map/jit(_take)/select_n | solution.py:190
  166.1 5.5 %all-to-all-start = ((bf16[8,128,512]{2,1,0:T(8,128)(2,1)}), bf16[8,128,512]{2,1,0:T(8,128)(2,1)}, u32[]{:S(2)}, u32[]{:S(2)}) async-start(bf16[8,128,512]{2,1,0:T(8,128)(2,1)} %broadcast_select_fusion), calls=%async_computation.1 | async-start | bytes 2097152 | tf_op jit(solution)/shard_map/all_to_all | solution.py:191
  171.6 0.6 dynamic_slice.15
  172.2 0.6 iota_compare_fusion.2
  172.8 0.0 copy-done.4
  172.8 0.0 copy-done.6
  172.9 0.1 select_reduce_fusion
  173.1 0.3 copy.48
  173.4 0.9 broadcast_select_fusion.2
  174.3 20.8 %all-to-all-done = bf16[8,128,512]{2,1,0:T(8,128)(2,1)} async-done(((bf16[8,128,512]{2,1,0:T(8,128)(2,1)}), bf16[8,128,512]{2,1,0:T(8,128)(2,1)}, u32[]{:S(2)}, u32[]{:S(2)}) %all-to-all-start) | async-done | bytes 1048608 | tf_op jit(solution)/shard_map/all_to_all | solution.py:191
  195.1 1.8 gather_fusion.1
  196.9 0.1 broadcast_select_fusion.1
  197.1 5.2 %all_to_all.20 = bf16[6,128,512]{2,1,0:T(8,128)(2,1)S(1)} all-to-all(bf16[6,128,512]{2,1,0:T(8,128)(2,1)S(1)} %broadcast_select_fusion.1), channel_id=1, replica_groups=mesh['replica'=2,'group'=8,'tensor'=2] {'tensor'}, dimensions={0} | all-to-all | bytes 1572864 | tf_op jit(solution)/shard_map/all_to_all | solution.py:193
  202.3 0.8 copy.47
  203.1 0.1 copy.56
  203.3 0.0 all-gather.5.cloned.1.call-done
  203.3 8.2 %convolution_convert_fusion = bf16[384,4096]{1,0:T(8,128)(2,1)} fusion(bf16[384,1024]{1,0:T(8,128)(2,1)S(1)} %bitcast.80, bf16[1024,4096]{1,0:T(8,128)(2,1)} %all-gather.5.cloned.1.call-done), kind=kOutput, calls=%fused_computation.6 | convolution fusion | flops 3222798336 | bytes 12320768 | tf_op jit(solution)/shard_map/dot_general | solution.py:194
  (9 shorter events, 0.1 us)
Async XLA Ops:
  8.0 1.2 copy-start
  8.0 117.1 %all-gather.3.cloned.1.call-start = ((), (), s32[]{:S(2)}) async-start(), calls=%async_computation.4 | async-start | bytes 4718592 | tf_op jit(solution)/shard_map/all_gather | solution.py:184
  10.1 82.4 %copy-start.2 = (f32[2048]{0:T(1024)S(1)}, f32[2048]{0:T(1024)}, u32[]{:S(2)}) copy-start(f32[2048]{0:T(1024)} %param.8) | copy-start | bytes 24580
  10.1 135.1 %reduce-scatter.2.cloned.1.call-start = ((), (), s32[]{:S(2)}) async-start(), calls=%async_computation.3 | async-start | bytes 9437184 | tf_op jit(solution)/shard_map/reduce_scatter | solution.py:148
  92.5 4.0 %copy-start.1 = (bf16[8,192,2048]{2,1,0:T(8,128)(2,1)S(1)}, bf16[8,192,2048]{2,1,0:T(8,128)(2,1)}, u32[]{:S(2)}) copy-start(bf16[8,192,2048]{2,1,0:T(8,128)(2,1)} %shard_map.86) | copy-start | bytes 18874372
  105.3 20.5 %copy-start.3 = (s32[8]{0:T(128)S(1)}, s32[8]{0:T(128)}, u32[]{:S(2)}) copy-start(s32[8]{0:T(128)} %param.11) | copy-start | bytes 100
  105.3 98.0 %all-gather.5.cloned.1.call-start = ((), (), s32[]{:S(2)}) async-start(), calls=%async_computation.5 | async-start | bytes 12582912 | tf_op jit(solution)/shard_map/all_gather | solution.py:185
  126.5 0.6 copy-start.5
  160.9 11.9 %copy-start.4 = (s32[8]{0:T(128)S(1)}, s32[8]{0:T(128)}, u32[]{:S(2)}) copy-start(s32[8]{0:T(128)} %get-tuple-element.3) | copy-start | bytes 100
  160.9 12.0 %copy-start.6 = (s32[8]{0:T(128)S(1)}, s32[8]{0:T(128)}, u32[]{:S(2)}) copy-start(s32[8]{0:T(128)} %copy-done.5) | copy-start | bytes 100
  166.1 29.0 %all-to-all-start = ((bf16[8,128,512]{2,1,0:T(8,128)(2,1)}), bf16[8,128,512]{2,1,0:T(8,128)(2,1)}, u32[]{:S(2)}, u32[]{:S(2)}) async-start(bf16[8,128,512]{2,1,0:T(8,128)(2,1)} %broadcast_select_fusion), calls=%async_computation.1 | async-start | bytes 2097152 | tf_op jit(solution)/shard_map/all_to_all | solution.py:191
Sparse Core Ops, SparseCore 0:
  11.7 113.3 all-gather.2
Sparse Core Ops, SparseCore 1:
  105.4 39.8 reduce-scatter.1
  146.7 20.9 all-gather.4

commit v3 on v1

--- a/solution.py
+++ b/solution.py
@@ -1,6 +1,9 @@
+import functools
 import jax
 import jax.numpy as jnp
 from jax import lax
+from jax.experimental import pallas as pl
+from jax.experimental.pallas import tpu as pltpu
 from jax.sharding import PartitionSpec as P
 
 HD = 128
@@ -35,6 +38,174 @@
     partial_sq = jnp.sum(floats * floats, axis=-1)
     summed = lax.psum(partial_sq, "tensor")
     return lax.rsqrt(summed / model_width + epsilon)
+
+
+class Spread:
+    def __init__(self, line, shard, rows, place, sems, local_sem, sibling_copies):
+        self.line, self.shard, self.place = line, shard, place
+        self.send_sem, self.recv_sem, self.local_sem = *sems, local_sem
+        self.half, self.quarter = rows // 2, rows // 4
+        self.rows, self.sibling_copies = rows, sibling_copies
+        self.pool = lax.axis_index("replica")
+        group, self.core = lax.axis_index("group"), lax.axis_index("tensor")
+        self.group, self.z, self.y = group, group // 2, group % 2
+        self.across = (1 - self.pool, group, self.core)
+        self.beside = (self.pool, self.z * 2 + (1 - self.y), self.core)
+        self.sibling = (self.pool, group, 1 - self.core)
+        self.count, self.all, self.kin = 0, [], []
+
+    def along(self, step, y):
+        return (self.z + step) % self.line * 2 + y
+
+    def peers(self):
+        spread = [(self.pool, self.along(d, self.y), self.core) for d in range(1, self.line)]
+        return spread + [self.across, self.beside]
+
+    def send(self, src, dst, peer):
+        copy = pltpu.make_async_remote_copy(
+            src_ref=src,
+            dst_ref=dst,
+            send_sem=self.send_sem.at[self.count],
+            recv_sem=self.recv_sem.at[self.count],
+            device_id=peer,
+            device_id_type=pl.DeviceIdType.MESH,
+        )
+        self.count += 1
+        copy.start()
+        self.all.append(copy)
+        return copy
+
+    def relay(self, source, begin, count, peer):
+        place = self.place(source, begin, count)
+        return self.send(place, place, peer)
+
+    def share(self, source, begin, count):
+        if self.sibling_copies:
+            self.kin.append(self.relay(source, begin, count, self.sibling))
+
+    def start(self):
+        mine = self.pool * self.half
+        src = self.shard.at[pl.ds(mine, self.half)]
+        dst = self.place(self.group, mine, self.half)
+        self.own = pltpu.make_async_copy(
+            self.shard, self.place(self.group, 0, self.rows), self.local_sem
+        )
+        self.own.start()
+        self.first = [
+            self.send(src, dst, (self.pool, self.along(d, self.y), self.core))
+            for d in range(1, self.line)
+        ]
+        self.sideways = [self.send(src, dst, self.beside)]
+        if self.sibling_copies:
+            whole = self.place(self.group, 0, self.rows)
+            self.kin.append(self.send(self.shard, whole, self.sibling))
+
+    def trade(self):
+        mine = self.pool * self.half
+        self.over = []
+        for d in range(1, self.line):
+            self.first[d - 1].wait_recv()
+            source = self.along(self.line - d, self.y)
+            self.over.append(self.relay(source, mine, self.half, self.across))
+            self.sideways.append(self.relay(source, mine, self.half, self.beside))
+            self.share(source, mine, self.half)
+
+    def finish(self):
+        mine, other = self.pool * self.half, (1 - self.pool) * self.half
+        second, third = [], []
+        for d in range(self.line):
+            self.sideways[d].wait_recv()
+            source = self.along(self.line - d, 1 - self.y)
+            skip = 0 if d == 0 else self.quarter
+            second.append(self.relay(source, mine + skip, self.half - skip, self.across))
+            self.share(source, mine, self.half)
+            if d > 0:
+                self.over[d - 1].wait_recv()
+                source = self.along(self.line - d, self.y)
+                third.append(self.relay(source, other, self.quarter, self.beside))
+                self.share(source, other, self.half)
+        self.second, self.third = second, third
+
+    def end(self):
+        other = (1 - self.pool) * self.half
+        for d in range(self.line):
+            skip = 0 if d == 0 else self.quarter
+            source = self.along(self.line - d, 1 - self.y)
+            self.second[d].wait_recv()
+            self.share(source, other + skip, self.half - skip)
+            if d > 0:
+                self.third[d - 1].wait_recv()
+                self.share(source, other, self.quarter)
+        for copy in self.kin:
+            copy.wait_recv()
+        for copy in self.all:
+            copy.wait_send()
+        self.own.wait()
+
+
+def copy_counts(line):
+    return 5 * line - 3, 10 * line - 5
+
+
+def gather_kernel(
+    line, rows_ref, cols_ref, rows_full, cols_full, own_sem, rsend, rrecv, csend, crecv
+):
+    core = lax.axis_index("tensor")
+    part, width = cols_ref.shape
+
+    def place_rows(source, begin, count):
+        return rows_full.at[source, pl.ds(begin, count)]
+
+    def place_cols(source, begin, count):
+        top = pl.multiple_of(core * part + begin, part // 4)
+        left = pl.multiple_of(source * width, width)
+        return cols_full.at[pl.ds(top, count), pl.ds(left, width)]
+
+    first = Spread(
+        line, rows_ref, rows_ref.shape[0], place_rows, (rsend, rrecv), own_sem.at[0], False
+    )
+    later = Spread(line, cols_ref, part, place_cols, (csend, crecv), own_sem.at[1], True)
+    barrier = pltpu.get_barrier_semaphore()
+    peers = first.peers() + [first.sibling]
+    for peer in peers:
+        pl.semaphore_signal(barrier, inc=1, device_id=peer, device_id_type=pl.DeviceIdType.MESH)
+    pl.semaphore_wait(barrier, len(peers))
+    first.start()
+    first.trade()
+    later.start()
+    first.finish()
+    later.trade()
+    later.finish()
+    first.end()
+    later.end()
+
+
+def gather_weights(rows, cols, group_size, tensor_size, collective_id):
+    line = group_size // 2
+    few, many = copy_counts(line)
+    any_space = pl.BlockSpec(memory_space=pl.ANY)
+    full, out_full = pl.pallas_call(
+        functools.partial(gather_kernel, line),
+        out_shape=(
+            jax.ShapeDtypeStruct((group_size,) + rows.shape, rows.dtype),
+            jax.ShapeDtypeStruct(
+                (tensor_size * cols.shape[0], group_size * cols.shape[1]), cols.dtype
+            ),
+        ),
+        in_specs=[any_space, any_space],
+        out_specs=(any_space, any_space),
+        scratch_shapes=[
+            pltpu.SemaphoreType.DMA((2,)),
+            pltpu.SemaphoreType.DMA((few,)),
+            pltpu.SemaphoreType.DMA((few,)),
+            pltpu.SemaphoreType.DMA((many,)),
+            pltpu.SemaphoreType.DMA((many,)),
+        ],
+        compiler_params=pltpu.CompilerParams(
+            collective_id=collective_id, has_side_effects=True
+        ),
+    )(rows, cols)
+    return full.reshape((-1,) + rows.shape[1:]), out_full
 
 
 def project_and_attend(hidden_in, norm_gain, rows_full, segments, tensor_size):
@@ -76,11 +247,14 @@
     source_of = jnp.sum(jnp.where(chosen, groups_iota[None, :], 0), axis=1)
     home_live = jnp.arange(slot_count, dtype=jnp.int32) < home_count[own_group]
     segments = lax.dynamic_slice_in_dim(segment_ids, own_group * slot_count, slot_count, 0)
-    rows_full = lax.all_gather(w_qkv, "group", axis=0, tiled=True)
     part_rows = w_out.shape[0] // tensor_size
     own_part = lax.dynamic_slice_in_dim(w_out, own_rank * part_rows, part_rows, 0)
-    out_part = lax.all_gather(own_part, "group", axis=1, tiled=True)
-    out_full = lax.all_gather(out_part, "tensor", axis=0, tiled=True)
+    if (lax.axis_size("replica"), group_size, tensor_size) == (2, 8, 2):
+        rows_full, out_full = gather_weights(w_qkv, own_part, group_size, tensor_size, 0)
+    else:
+        rows_full = lax.all_gather(w_qkv, "group", axis=0, tiled=True)
+        out_part = lax.all_gather(own_part, "group", axis=1, tiled=True)
+        out_full = lax.all_gather(out_part, "tensor", axis=0, tiled=True)
     context, cache = project_and_attend(
         hidden_in, norm_gain, rows_full, segments, tensor_size
     )

time: 278 us -> 230 us (0.83)
  waiting for transfers between devices: 190 us -> 39.9 us
  Pallas kernels: 0 us -> 103 us
    all_gather x3 -> x0, waiting for transfers between devices: 157 us -> none  [the longest x1 93.4 us: per_device(): rows_full = lax.all_gather(w_qkv, 'group', axis=0, tiled=True)]
    pallas_call x0 -> x1, Pallas kernels: none -> 103 us  [gather_weights(): pl.pallas_call(functools.partial(gather_kernel, line), out_shape=(jax.Sha...]
    reduce_scatter x1, waiting for transfers between devices: 10.5 us -> 18.9 us  [project_and_attend(): lax.psum_scatter(partial, 'tensor', scatter_dimension=1, tiled=True)]
  transfers between devices with their start and end apart: 5 -> 2, of which waited for: 4 -> 2; matrix products, arithmetic and copies ran while one was open for 17% -> 3% of each run, Pallas kernels for 0% -> 0%
where the time goes in v3:
time: 230 us; the launch traced here: 226 us
  Pallas kernels  103 us (45%)
  waiting for transfers between devices  39.9 us (17%)
  matrix products  23.3 us (10%)
  local copies, waits for them, and re-layouts  18.2 us (8%)
  between operations  14.9 us (6%)
  other arithmetic  14.4 us (6%)
  blocking collectives  7.43 us (3%)
  starting transfers between devices  5.53 us (2%)
    pallas_call x1, Pallas kernels, gather_weights(): pl.pallas_call(functools.partial(gather_kernel, line), out_shape=(jax.Sha...  103 us
    all_to_all x1, waiting for transfers between devices, per_device(): lax.all_to_all(outgoing, 'group', split_axis=0, concat_axis=0, tiled=True)  21 us
    reduce_scatter x1, waiting for transfers between devices, project_and_attend(): lax.psum_scatter(partial, 'tensor', scatter_dimension=1, tiled=True)  18.9 us
    dot_general x1, matrix products, project_and_attend(): lax.dot_general(scaled, rows_full, contract, preferred_element_type=jnp.f...  11.8 us
    dot_general x1, matrix products, per_device(): jnp.dot(rows.reshape(local_blocks * block_len, -1), out_full, preferred_e...  8.21 us
    all_to_all x1, starting transfers between devices, per_device(): lax.all_to_all(outgoing, 'group', split_axis=0, concat_axis=0, tiled=True)  5.49 us
    reduce_sum x1, other arithmetic, row_scale(): partial_sq = jnp.sum(floats * floats, axis=-1)  5.44 us
    all_to_all x1, blocking collectives, per_device(): lax.all_to_all(helped, 'tensor', split_axis=0, concat_axis=2, tiled=True)  4.98 us
  transfers between devices with their start and end apart: 2, of which 2 were waited for; matrix products, arithmetic and copies ran while one was open for 3% of the time, Pallas kernels for 0%

profile of v3, /device:TPU:9, one launch (start us, length us, event | category | flops | bytes accessed | tf_op | source)
XLA Modules:
  0.0 226.4 jit_solution(9591042821983275113)
XLA Ops:
  7.2 0.0 copy-start
  7.2 0.0 reduce-scatter.2.cloned.1.call-start
  7.2 5.4 %fusion.1 = (f32[8,128]{1,0:T(8,128)S(1)}, bf16[8,128,2048]{2,1,0:T(8,128)(2,1)}) fusion(bf16[8,128,2048]{2,1,0:T(8,128)(2,1)} %param.7, f32[2048]{0:T(1024)} %param.8), kind=kLoop, calls=%fused_computation.5 | loop fusion | flops 10484736 | bytes 8400896 | tf_op jit(solution)/shard_map/reduce_sum | solution.py:38
  12.7 0.0 copy-done
  12.7 0.8 constant_dynamic-slice_fusion.1.cols_ref
  13.5 102.8 %shard_map.86 = (bf16[8,192,2048]{2,1,0:T(8,128)(2,1)}, bf16[1024,4096]{1,0:T(8,128)(2,1)}) custom-call(bf16[192,2048]{1,0:T(8,128)(2,1)} %rows_ref.1, bf16[512,512]{1,0:T(8,128)(2,1)} %constant_dynamic-slice_fusion.1.cols_ref), custom_call_target="tpu_custom_call" | custom-call | tf_op jit(solution)/shard_map/pallas_call | solution.py:187
  116.3 11.8 %fusion.17 = f32[1024,1536]{1,0:T(8,128)} fusion(bf16[1024,2048]{1,0:T(8,128)(2,1)} %bitcast.74, bf16[1536,2048]{1,0:T(8,128)(2,1)} %bitcast.81), kind=kOutput, calls=%fused_computation.61 | convolution fusion | flops 6442450944 | bytes 16777216 | tf_op jit(solution)/shard_map/dot_general | solution.py:217
  128.1 0.0 copy-start.1
  128.1 0.0 reduce-scatter.2.cloned.1.call-update
  128.8 0.0 copy-done.1
  128.8 0.2 reduce-window.9
  129.0 0.5 fusion.14
  129.5 0.0 copy-start.3
  129.5 0.6 dynamic_slice.12
  130.1 0.0 copy-done.3
  130.1 2.5 %psum.7 = f32[8,128]{1,0:T(8,128)S(1)} all-reduce(f32[8,128]{1,0:T(8,128)S(1)} %get-tuple-element.9), channel_id=1, replica_groups=mesh['replica'=2,'group'=8,'tensor'=2] {'tensor'}, use_global_device_ids=true, to_apply=%region_4.5 | all-reduce | flops 1024 | bytes 8192 | tf_op jit(solution)/shard_map/psum | solution.py:39
  132.6 0.7 fusion.12
  133.2 0.7 compare_and_fusion.1
  133.9 0.7 constant_dynamic-slice_fusion
  134.6 0.2 compare_and_fusion
  134.9 18.9 %reduce-scatter.2.cloned.1.call-done = f32[1024,768]{1,0:T(8,128)} async-done(((f32[1024,1536]{1,0:T(8,128)}), f32[1024,768]{1,0:T(8,128)}) %reduce-scatter.2.cloned.1.call-update) | async-done | bytes 3145744 | tf_op jit(solution)/shard_map/reduce_scatter | solution.py:220
  153.7 2.1 multiply_convert_fusion
  155.9 1.6 copy.41
  157.5 1.8 copy.55
  159.3 1.0 slice.22
  160.4 2.4 %copy.54 = bf16[8,128,1,4,128]{4,1,3,0,2:T(8,128)(2,1)} copy(bf16[8,128,1,4,128]{1,0,4,3,2:T(8,128)(2,1)} %slice.22) | data formatting | bytes 2097152
  162.9 0.2 copy.53
  163.1 1.7 fusion.16
  164.8 0.4 fusion.2
  165.2 1.6 convolution_convert_fusion.1
  166.8 2.3 %copy.46 = bf16[8,128,512]{2,1,0:T(8,128)(2,1)} copy(bf16[8,128,512]{1,2,0:T(8,128)(2,1)} %bitcast.78) | data formatting | bytes 2097152 | tf_op jit(solution)/shard_map/reshape;reshape | solution.py:223
  169.1 0.0 copy-start.2
  169.1 0.0 copy-start.4
  169.2 2.8 %gather_fusion = bf16[8,128,512]{2,1,0:T(8,128)(2,1)} fusion(bf16[8,128,512]{2,1,0:T(8,128)(2,1)} %copy.46, s32[1024]{0:T(1024)S(1)} %pad_clamp_fusion.1), kind=kCustom, calls=%fused_computation | custom fusion | bytes 2097184 | tf_op jit(solution)/shard_map/jit(_take)/gather | solution.py:262
  172.0 2.4 %broadcast_select_fusion = bf16[8,128,512]{2,1,0:T(8,128)(2,1)} fusion(bf16[8,128,512]{2,1,0:T(8,128)(2,1)} %gather_fusion, pred[8]{0:T(512)(128)(4,1)S(1)} %compare_and_fusion.1), kind=kLoop, calls=%fused_computation.15 | loop fusion | flops 524288 | bytes 2097160 | tf_op jit(solution)/shard_map/jit(_take)/select_n | solution.py:262
  174.3 5.5 %all-to-all-start = ((bf16[8,128,512]{2,1,0:T(8,128)(2,1)}), bf16[8,128,512]{2,1,0:T(8,128)(2,1)}, u32[]{:S(2)}, u32[]{:S(2)}) async-start(bf16[8,128,512]{2,1,0:T(8,128)(2,1)} %broadcast_select_fusion), calls=%async_computation.1 | async-start | bytes 2097152 | tf_op jit(solution)/shard_map/all_to_all | solution.py:263
  179.8 0.6 dynamic_slice.15
  180.4 0.6 iota_compare_fusion.2
  181.0 0.0 copy-done.2
  181.1 0.0 copy-done.4
  181.1 0.1 select_reduce_fusion
  181.3 0.3 copy.48
  181.6 0.9 broadcast_select_fusion.2
  182.5 21.0 %all-to-all-done = bf16[8,128,512]{2,1,0:T(8,128)(2,1)} async-done(((bf16[8,128,512]{2,1,0:T(8,128)(2,1)}), bf16[8,128,512]{2,1,0:T(8,128)(2,1)}, u32[]{:S(2)}, u32[]{:S(2)}) %all-to-all-start) | async-done | bytes 1048608 | tf_op jit(solution)/shard_map/all_to_all | solution.py:263
  203.5 1.8 gather_fusion.1
  205.3 0.1 broadcast_select_fusion.1
  205.5 5.0 %all_to_all.20 = bf16[6,128,512]{2,1,0:T(8,128)(2,1)S(1)} all-to-all(bf16[6,128,512]{2,1,0:T(8,128)(2,1)S(1)} %broadcast_select_fusion.1), channel_id=1, replica_groups=mesh['replica'=2,'group'=8,'tensor'=2] {'tensor'}, dimensions={0} | all-to-all | bytes 1572864 | tf_op jit(solution)/shard_map/all_to_all | solution.py:265
  210.4 0.8 copy.47
  211.2 0.1 copy.56
  211.4 8.2 %convolution_convert_fusion = bf16[384,4096]{1,0:T(8,128)(2,1)} fusion(bf16[384,1024]{1,0:T(8,128)(2,1)S(1)} %bitcast.79, bf16[1024,4096]{1,0:T(8,128)(2,1)} %get-tuple-element.5), kind=kOutput, calls=%fused_computation.6 | convolution fusion | flops 3222798336 | bytes 12320768 | tf_op jit(solution)/shard_map/dot_general | solution.py:266
  (9 shorter events, 0.1 us)
Async XLA Ops:
  7.2 5.5 %copy-start = (bf16[1024,512]{1,0:T(8,128)(2,1)S(1)}, bf16[1024,512]{1,0:T(8,128)(2,1)}, u32[]{:S(2)}) copy-start(bf16[1024,512]{1,0:T(8,128)(2,1)} %param.10) | copy-start | bytes 3145732
  7.2 146.6 %reduce-scatter.2.cloned.1.call-start = ((), (), s32[]{:S(2)}) async-start(), calls=%async_computation.3 | async-start | bytes 9437184 | tf_op jit(solution)/shard_map/reduce_scatter | solution.py:220
  128.1 0.7 copy-start.1
  129.5 0.6 copy-start.3
  169.1 11.9 %copy-start.2 = (s32[8]{0:T(128)S(1)}, s32[8]{0:T(128)}, u32[]{:S(2)}) copy-start(s32[8]{0:T(128)} %get-tuple-element.7) | copy-start | bytes 100
  169.1 11.9 %copy-start.4 = (s32[8]{0:T(128)S(1)}, s32[8]{0:T(128)}, u32[]{:S(2)}) copy-start(s32[8]{0:T(128)} %copy-done.3) | copy-start | bytes 100
  174.3 29.2 %all-to-all-start = ((bf16[8,128,512]{2,1,0:T(8,128)(2,1)}), bf16[8,128,512]{2,1,0:T(8,128)(2,1)}, u32[]{:S(2)}, u32[]{:S(2)}) async-start(bf16[8,128,512]{2,1,0:T(8,128)(2,1)} %broadcast_select_fusion), calls=%async_computation.1 | async-start | bytes 2097152 | tf_op jit(solution)/shard_map/all_to_all | solution.py:263
Sparse Core Ops, SparseCore 0:
  128.3 25.4 reduce-scatter.1

commit v4 on v3

--- a/solution.py
+++ b/solution.py
@@ -147,68 +147,186 @@
     return 5 * line - 3, 10 * line - 5
 
 
-def gather_kernel(
-    line, rows_ref, cols_ref, rows_full, cols_full, own_sem, rsend, rrecv, csend, crecv
-):
-    core = lax.axis_index("tensor")
-    part, width = cols_ref.shape
-
-    def place_rows(source, begin, count):
-        return rows_full.at[source, pl.ds(begin, count)]
-
-    def place_cols(source, begin, count):
-        top = pl.multiple_of(core * part + begin, part // 4)
-        left = pl.multiple_of(source * width, width)
-        return cols_full.at[pl.ds(top, count), pl.ds(left, width)]
-
-    first = Spread(
-        line, rows_ref, rows_ref.shape[0], place_rows, (rsend, rrecv), own_sem.at[0], False
-    )
-    later = Spread(line, cols_ref, part, place_cols, (csend, crecv), own_sem.at[1], True)
+def greet(peers):
     barrier = pltpu.get_barrier_semaphore()
-    peers = first.peers() + [first.sibling]
     for peer in peers:
         pl.semaphore_signal(barrier, inc=1, device_id=peer, device_id_type=pl.DeviceIdType.MESH)
     pl.semaphore_wait(barrier, len(peers))
-    first.start()
-    first.trade()
-    later.start()
-    first.finish()
-    later.trade()
-    later.finish()
-    first.end()
-    later.end()
-
-
-def gather_weights(rows, cols, group_size, tensor_size, collective_id):
+
+
+def gather_kernel(line, rows_ref, rows_full, own_sem, rsend, rrecv):
+    def place_rows(source, begin, count):
+        return rows_full.at[source, pl.ds(begin, count)]
+
+    spread = Spread(
+        line, rows_ref, rows_ref.shape[0], place_rows, (rsend, rrecv), own_sem, False
+    )
+    greet(spread.peers())
+    spread.start()
+    spread.trade()
+    spread.finish()
+    spread.end()
+
+
+def gather_rows(rows, group_size, collective_id):
     line = group_size // 2
-    few, many = copy_counts(line)
+    few, _ = copy_counts(line)
     any_space = pl.BlockSpec(memory_space=pl.ANY)
-    full, out_full = pl.pallas_call(
+    full = pl.pallas_call(
         functools.partial(gather_kernel, line),
-        out_shape=(
-            jax.ShapeDtypeStruct((group_size,) + rows.shape, rows.dtype),
-            jax.ShapeDtypeStruct(
-                (tensor_size * cols.shape[0], group_size * cols.shape[1]), cols.dtype
-            ),
-        ),
-        in_specs=[any_space, any_space],
-        out_specs=(any_space, any_space),
+        out_shape=jax.ShapeDtypeStruct((group_size,) + rows.shape, rows.dtype),
+        in_specs=[any_space],
+        out_specs=any_space,
         scratch_shapes=[
-            pltpu.SemaphoreType.DMA((2,)),
+            pltpu.SemaphoreType.DMA,
             pltpu.SemaphoreType.DMA((few,)),
             pltpu.SemaphoreType.DMA((few,)),
-            pltpu.SemaphoreType.DMA((many,)),
-            pltpu.SemaphoreType.DMA((many,)),
         ],
         compiler_params=pltpu.CompilerParams(
             collective_id=collective_id, has_side_effects=True
         ),
-    )(rows, cols)
-    return full.reshape((-1,) + rows.shape[1:]), out_full
-
-
-def project_and_attend(hidden_in, norm_gain, rows_full, segments, tensor_size):
+    )(rows)
+    return full.reshape((-1,) + rows.shape[1:])
+
+
+def attend_one(projected, bias):
+    block_len = projected.shape[0]
+    heads = [projected[:, i * HD : (i + 1) * HD] for i in range(Q_PER + 2)]
+    queries = jnp.concatenate(heads[:Q_PER], axis=0)
+    scores = lax.dot_general(
+        queries, heads[Q_PER], (((1,), (1,)), ((), ())), preferred_element_type=jnp.float32
+    ) * HD ** (-0.5)
+    scores = scores.reshape(Q_PER, block_len, block_len) + bias[None]
+    raised = jnp.exp(scores - jnp.max(scores, axis=-1, keepdims=True))
+    weights = (raised / jnp.sum(raised, axis=-1, keepdims=True)).astype(jnp.bfloat16)
+    context = jnp.dot(
+        weights.reshape(Q_PER * block_len, block_len),
+        heads[Q_PER + 1],
+        preferred_element_type=jnp.float32,
+    ).astype(jnp.bfloat16)
+    parts = [context[i * block_len : (i + 1) * block_len] for i in range(Q_PER)]
+    return jnp.concatenate(parts, axis=1)
+
+
+def tail_kernel(
+    line, slots_ref, source_ref, proj_ref, bias_ref, cols_ref, out_ref,
+    w_full, made, got, rows_buf,
+    own_sem, csend, crecv, bsend, brecv, ksend, krecv,
+):
+    groups = 2 * line
+    pool, group = lax.axis_index("replica"), lax.axis_index("group")
+    core = lax.axis_index("tensor")
+    part, width = cols_ref.shape
+
+    def place_cols(source, begin, count):
+        top = pl.multiple_of(core * part + begin, part // 4)
+        left = pl.multiple_of(source * width, width)
+        return w_full.at[pl.ds(top, count), pl.ds(left, width)]
+
+    spread = Spread(line, cols_ref, part, place_cols, (csend, crecv), own_sem, True)
+
+    def block_copy(step):
+        return pltpu.make_async_remote_copy(
+            src_ref=made.at[step],
+            dst_ref=got.at[group, core],
+            send_sem=bsend.at[step],
+            recv_sem=brecv.at[step],
+            device_id=(pool, (group + step) % groups, core),
+            device_id_type=pl.DeviceIdType.MESH,
+        )
+
+    def kin_copy(step):
+        place = got.at[(group + groups - step) % groups, core]
+        return pltpu.make_async_remote_copy(
+            src_ref=place,
+            dst_ref=place,
+            send_sem=ksend.at[step],
+            recv_sem=krecv.at[step],
+            device_id=(pool, group, 1 - core),
+            device_id_type=pl.DeviceIdType.MESH,
+        )
+
+    others = [(pool, (group + d) % groups, core) for d in range(1, groups)]
+    greet(others + [spread.across, spread.sibling])
+    spread.start()
+
+    def attend_and_send(step, carry):
+        slot = slots_ref[(group + step) % groups]
+        made[step] = attend_one(proj_ref[slot], bias_ref[slot])
+        block_copy(step).start()
+        return carry
+
+    lax.fori_loop(1, groups, attend_and_send, 0)
+    slot = slots_ref[group]
+    got[group, core] = attend_one(proj_ref[slot], bias_ref[slot])
+    kin_copy(0).start()
+    spread.trade()
+    spread.finish()
+
+    def pass_on(step, carry):
+        block_copy(step).wait_recv()
+        kin_copy(step).start()
+        return carry
+
+    lax.fori_loop(1, groups, pass_on, 0)
+    spread.end()
+
+    def settle(step, carry):
+        kin_copy(step).wait()
+        return carry
+
+    def settle_sent(step, carry):
+        block_copy(step).wait_send()
+        return carry
+
+    lax.fori_loop(0, groups, settle, 0)
+    lax.fori_loop(1, groups, settle_sent, 0)
+    block_len, wide = made.shape[1:]
+    for b in range(out_ref.shape[0] // block_len):
+        block = got[source_ref[b]]
+        for c in range(got.shape[1]):
+            rows_buf[b * block_len : (b + 1) * block_len, c * wide : (c + 1) * wide] = block[c]
+
+    def column_tile(tile, carry):
+        columns = pl.ds(pl.multiple_of(tile * width, width), width)
+        out_ref[:, columns] = jnp.dot(
+            rows_buf[...], w_full[:, columns], preferred_element_type=jnp.float32
+        ).astype(jnp.bfloat16)
+        return carry
+
+    lax.fori_loop(0, groups, column_tile, 0)
+
+
+def attend_and_mix(slots, sources, projected, bias, cols, group_size, tensor_size):
+    line = group_size // 2
+    _, many = copy_counts(line)
+    block_len = projected.shape[1]
+    wide = Q_PER * HD
+    depth, model_width = tensor_size * cols.shape[0], group_size * cols.shape[1]
+    tokens = sources.shape[0] * block_len
+    smem, vmem = (pl.BlockSpec(memory_space=m) for m in (pltpu.SMEM, pltpu.VMEM))
+    return pl.pallas_call(
+        functools.partial(tail_kernel, line),
+        out_shape=jax.ShapeDtypeStruct((tokens, model_width), jnp.bfloat16),
+        in_specs=[smem, smem, vmem, vmem, pl.BlockSpec(memory_space=pl.ANY)],
+        out_specs=vmem,
+        scratch_shapes=[
+            pltpu.VMEM((depth, model_width), jnp.bfloat16),
+            pltpu.VMEM((group_size, block_len, wide), jnp.bfloat16),
+            pltpu.VMEM((group_size, tensor_size, block_len, wide), jnp.bfloat16),
+            pltpu.VMEM((tokens, tensor_size * wide), jnp.bfloat16),
+            pltpu.SemaphoreType.DMA,
+            pltpu.SemaphoreType.DMA((many,)),
+            pltpu.SemaphoreType.DMA((many,)),
+        ]
+        + [pltpu.SemaphoreType.DMA((group_size,))] * 4,
+        compiler_params=pltpu.CompilerParams(
+            collective_id=1, has_side_effects=True, vmem_limit_bytes=48 * 2**20
+        ),
+    )(slots, sources, projected, bias, cols)
+
+
+def project(hidden_in, norm_gain, rows_full, tensor_size):
     slot_count, block_len, features = hidden_in.shape
     floats = hidden_in.astype(jnp.float32)
     scale = row_scale(floats, features * tensor_size).reshape(-1)
@@ -219,10 +337,7 @@
     )
     summed = lax.psum_scatter(partial, "tensor", scatter_dimension=1, tiled=True)
     projected = (summed * scale[:, None]).astype(jnp.bfloat16)
-    projected = projected.reshape(slot_count, block_len, -1, Q_PER + 2, HD)
-    context = attend(projected, segments).reshape(slot_count, block_len, -1)
-    cache = projected[:, :, :, Q_PER:].reshape(slot_count, block_len, -1)
-    return context, cache
+    return projected.reshape(slot_count, block_len, -1)
 
 
 def per_device(hidden_in, norm_gain, w_qkv, w_out, home_count, helper_start, segment_ids):
@@ -249,17 +364,31 @@
     segments = lax.dynamic_slice_in_dim(segment_ids, own_group * slot_count, slot_count, 0)
     part_rows = w_out.shape[0] // tensor_size
     own_part = lax.dynamic_slice_in_dim(w_out, own_rank * part_rows, part_rows, 0)
-    if (lax.axis_size("replica"), group_size, tensor_size) == (2, 8, 2):
-        rows_full, out_full = gather_weights(w_qkv, own_part, group_size, tensor_size, 0)
+    by_kernel = (lax.axis_size("replica"), group_size, tensor_size) == (2, 8, 2)
+    if by_kernel:
+        rows_full = gather_rows(w_qkv, group_size, 0)
     else:
         rows_full = lax.all_gather(w_qkv, "group", axis=0, tiled=True)
-        out_part = lax.all_gather(own_part, "group", axis=1, tiled=True)
-        out_full = lax.all_gather(out_part, "tensor", axis=0, tiled=True)
-    context, cache = project_and_attend(
-        hidden_in, norm_gain, rows_full, segments, tensor_size
-    )
+    projected = project(hidden_in, norm_gain, rows_full, tensor_size)
+    by_head = projected.reshape(slot_count, block_len, -1, Q_PER + 2, HD)
+    cache = by_head[:, :, :, Q_PER:].reshape(slot_count, block_len, -1)
     kv_cache = jnp.where(home_live[:, None, None], cache, jnp.zeros_like(cache))
-    outgoing = jnp.take(context, jnp.minimum(send_slot, slot_count - 1), axis=0)
+    slots = jnp.minimum(send_slot, slot_count - 1)
+    if by_kernel:
+        positions = jnp.arange(block_len)
+        allowed = (positions[:, None] >= positions[None, :])[None] & (
+            segments[:, :, None] == segments[:, None, :]
+        )
+        bias = jnp.where(allowed, 0.0, -jnp.inf).astype(jnp.float32)
+        sources = lax.dynamic_slice_in_dim(source_of, own_rank * local_blocks, local_blocks)
+        mixed = attend_and_mix(
+            slots, sources, projected, bias, own_part, group_size, tensor_size
+        )
+        return (mixed.reshape(local_blocks, block_len, -1), kv_cache)
+    out_part = lax.all_gather(own_part, "group", axis=1, tiled=True)
+    out_full = lax.all_gather(out_part, "tensor", axis=0, tiled=True)
+    context = attend(by_head, segments).reshape(slot_count, block_len, -1)
+    outgoing = jnp.take(context, slots, axis=0)
     arrived = lax.all_to_all(outgoing, "group", split_axis=0, concat_axis=0, tiled=True)
     helped = jnp.take(arrived, source_of, axis=0)
     rows = lax.all_to_all(helped, "tensor", split_axis=0, concat_axis=2, tiled=True)

time: 230 us -> 200 us (0.87); the launches traced: 226 us -> 200 us
  Pallas kernels: 103 us -> 136 us
  waiting for transfers between devices: 39.9 us -> 15.5 us
  matrix products: 23.3 us -> 8.64 us
  local copies, waits for them, and re-layouts: 18.2 us -> 12.3 us
  other arithmetic: 14.4 us -> 8.51 us
  starting transfers between devices: 5.53 us -> 0.04 us
  blocking collectives: 7.43 us -> 4.19 us
    pallas_call x1 -> x2, Pallas kernels: 103 us -> 136 us  [the longest x1 68.2 us: attend_and_mix(): pl.pallas_call(functools.partial(tail_kernel, line), out_shape=jax.ShapeD...]
    all_to_all x1 -> x0, waiting for transfers between devices: 21 us -> none  [per_device(): lax.all_to_all(outgoing, 'group', split_axis=0, concat_axis=0, tiled=True)]
    dot_general x4 -> x1, matrix products: 23.3 us -> 8.64 us  [project(): lax.dot_general(scaled, rows_full, contract, preferred_element_type=jnp.f...]
    all_to_all x1 -> x0, starting transfers between devices: 5.49 us -> none  [per_device(): lax.all_to_all(outgoing, 'group', split_axis=0, concat_axis=0, tiled=True)]
    all_to_all x1 -> x0, blocking collectives: 4.98 us -> none  [per_device(): lax.all_to_all(helped, 'tensor', split_axis=0, concat_axis=2, tiled=True)]
    gather x2 -> x0, local copies, waits for them, and re-layouts: 4.63 us -> none  [the longest x1 2.81 us: per_device(): outgoing = jnp.take(context, jnp.minimum(send_slot, slot_count - 1), axis=0)]
    reduce_scatter x1, waiting for transfers between devices: 18.9 us -> 15.5 us  [project(): lax.psum_scatter(partial, 'tensor', scatter_dimension=1, tiled=True)]
    select_n x4 -> x1, other arithmetic: 3.16 us -> 0.21 us  [per_device(): bias = jnp.where(allowed, 0.0, -jnp.inf).astype(jnp.float32)]
  transfers between devices with their start and end apart: 2 -> 1, of which waited for: 2 -> 1; matrix products, arithmetic and copies ran while one was open for 3% -> 2% of each run, Pallas kernels for 0% -> 0%
where the time goes in v4:
time: 200 us
  Pallas kernels  136 us (68%)
  waiting for transfers between devices  15.5 us (8%)
  between operations  14.8 us (7%)
  local copies, waits for them, and re-layouts  12.3 us (6%)
  matrix products  8.64 us (4%)
  other arithmetic  8.51 us (4%)
  blocking collectives  4.19 us (2%)
    pallas_call x1, Pallas kernels, attend_and_mix(): pl.pallas_call(functools.partial(tail_kernel, line), out_shape=jax.ShapeD...  68.2 us
    pallas_call x1, Pallas kernels, gather_rows(): pl.pallas_call(functools.partial(gather_kernel, line), out_shape=jax.Shap...  67.9 us
    reduce_scatter x1, waiting for transfers between devices, project(): lax.psum_scatter(partial, 'tensor', scatter_dimension=1, tiled=True)  15.5 us
    dot_general x1, matrix products, project(): lax.dot_general(scaled, rows_full, contract, preferred_element_type=jnp.f...  8.64 us
    unnamed x16, local copies, waits for them, and re-layouts  7.46 us
    psum x1, blocking collectives, row_scale(): summed = lax.psum(partial_sq, 'tensor')  4.19 us
  transfers between devices with their start and end apart: 1, of which 1 were waited for; matrix products, arithmetic and copies ran while one was open for 2% of the time, Pallas kernels for 0%

profile of v4, /device:TPU:9, one launch (start us, length us, event | category | flops | bytes accessed | tf_op | source)
XLA Modules:
  0.0 200.0 jit_solution(781857558693722814)
XLA Ops:
  7.2 0.0 copy-start
  7.2 0.0 copy-start.5
  7.2 0.0 reduce-scatter.2.cloned.1.call-start
  7.2 67.9 %shard_map.86 = bf16[8,192,2048]{2,1,0:T(8,128)(2,1)} custom-call(bf16[192,2048]{1,0:T(8,128)(2,1)} %rows_ref.1), custom_call_target="tpu_custom_call" | custom-call | tf_op jit(solution)/shard_map/pallas_call | solution.py:175
  75.1 0.0 copy-done.5
  75.1 0.0 copy-start.3
  75.1 3.6 %fusion.1 = (f32[8,128]{1,0:T(8,128)S(1)}, bf16[8,128,2048]{2,1,0:T(8,128)(2,1)S(1)}) fusion(bf16[8,128,2048]{2,1,0:T(8,128)(2,1)} %param.7, f32[2048]{0:T(1024)S(1)} %copy-done.5), kind=kLoop, calls=%fused_computation.3 | loop fusion | flops 10484736 | bytes 8400896 | tf_op jit(solution)/shard_map/reduce_sum | solution.py:38
  78.8 0.4 copy-done.3
  79.2 8.6 %fusion.7 = f32[1024,1536]{1,0:T(8,128)} fusion(bf16[1024,2048]{1,0:T(8,128)(2,1)S(1)} %bitcast.27, bf16[1536,2048]{1,0:T(8,128)(2,1)S(1)} %bitcast.25), kind=kOutput, calls=%fused_computation.30 | convolution fusion | flops 6442450944 | bytes 16777216 | tf_op jit(solution)/shard_map/dot_general | solution.py:335
  87.8 0.0 copy-start.6
  87.8 0.0 reduce-scatter.2.cloned.1.call-update
  88.5 0.0 copy-done.6
  88.5 0.2 reduce-window.9
  88.7 0.6 dynamic_slice.19
  89.3 0.6 dynamic_slice.15
  89.9 0.1 select_reduce_fusion
  90.0 0.1 dynamic_slice.16.source_ref
  90.1 4.2 %psum.7 = f32[8,128]{1,0:T(8,128)S(1)} all-reduce(f32[8,128]{1,0:T(8,128)S(1)} %get-tuple-element.5), channel_id=1, replica_groups=mesh['replica'=2,'group'=8,'tensor'=2] {'tensor'}, use_global_device_ids=true, to_apply=%region_4.5 | all-reduce | flops 1024 | bytes 8192 | tf_op jit(solution)/shard_map/psum | solution.py:39
  94.3 0.6 iota_compare_fusion.2
  94.9 0.7 fusion.3.slots_ref
  95.6 0.7 constant_dynamic-slice_fusion
  96.3 0.0 copy-done
  96.3 0.8 constant_dynamic-slice_fusion.1.cols_ref
  97.2 0.2 and_select_fusion.bias_ref
  97.4 15.5 %reduce-scatter.2.cloned.1.call-done = f32[1024,768]{1,0:T(8,128)} async-done(((f32[1024,1536]{1,0:T(8,128)}), f32[1024,768]{1,0:T(8,128)}) %reduce-scatter.2.cloned.1.call-update) | async-done | bytes 3145744 | tf_op jit(solution)/shard_map/reduce_scatter | solution.py:338
  112.9 2.1 %multiply_convert_fusion = bf16[1024,768]{1,0:T(8,128)(2,1)S(1)} fusion(f32[1024,768]{1,0:T(8,128)} %reduce-scatter.2.cloned.1.call-done, f32[1024]{0:T(1024)S(1)} %rsqrt_bitcast_fusion), kind=kLoop, calls=%fused_computation.4 | loop fusion | flops 1572864 | bytes 4722688 | tf_op jit(solution)/shard_map/convert_element_type | solution.py:339
  115.0 1.6 copy.11
  116.6 0.0 copy-start.2
  116.6 1.0 copy-done.2
  117.7 0.0 copy-start.4
  117.7 68.2 %shard_map.87 = bf16[384,4096]{1,0:T(8,128)(2,1)S(1)} custom-call(s32[8]{0:T(128)S(1)} %fusion.3.slots_ref, s32[3]{0:T(128)S(1)} %dynamic_slice.16.source_ref, bf16[8,128,768]{2,1,0:T(8,128)(2,1)S(1)} %bitcast.23, f32[8,128,128]{2,1,0:T(8,128)S(1)} %and_select_fusion.bias_ref, bf16[512,512]{1,0:T(8,128)(2,1)S(1)} %copy-done.2), custom_call_target="tpu_custom_call" | custom-call | tf_op jit(solution)/shard_map/pallas_call | solution.py:308
  185.9 0.0 copy-start.1
  185.9 1.7 copy-done.1
  187.6 0.0 copy-done.4
  187.6 0.4 copy.13
  188.1 0.3 copy.12
  188.4 0.9 broadcast_select_fusion
  189.3 3.9 %copy.16 = bf16[3,128,4096]{2,1,0:T(8,128)(2,1)} copy(bf16[3,128,4096]{2,1,0:T(8,128)(2,1)} %bitcast.24) | data formatting | bytes 6291456
  (5 shorter events, 0.1 us)
Async XLA Ops:
  7.2 89.2 %copy-start = (bf16[1024,512]{1,0:T(8,128)(2,1)S(1)}, bf16[1024,512]{1,0:T(8,128)(2,1)}, u32[]{:S(2)}) copy-start(bf16[1024,512]{1,0:T(8,128)(2,1)} %param.10) | copy-start | bytes 3145732
  7.2 67.9 %copy-start.5 = (f32[2048]{0:T(1024)S(1)}, f32[2048]{0:T(1024)}, u32[]{:S(2)}) copy-start(f32[2048]{0:T(1024)} %param.8) | copy-start | bytes 24580
  7.2 105.7 %reduce-scatter.2.cloned.1.call-start = ((), (), s32[]{:S(2)}) async-start(), calls=%async_computation.1 | async-start | bytes 9437184 | tf_op jit(solution)/shard_map/reduce_scatter | solution.py:338
  75.1 4.0 %copy-start.3 = (bf16[8,192,2048]{2,1,0:T(8,128)(2,1)S(1)}, bf16[8,192,2048]{2,1,0:T(8,128)(2,1)}, u32[]{:S(2)}) copy-start(bf16[8,192,2048]{2,1,0:T(8,128)(2,1)} %shard_map.86) | copy-start | bytes 18874372
  87.8 0.7 copy-start.6
  116.6 1.0 copy-start.2
  117.7 69.9 %copy-start.4 = (bf16[1024,768]{0,1:T(8,128)(2,1)S(1)}, bf16[1024,768]{0,1:T(8,128)(2,1)}, u32[]{:S(2)}) copy-start(bf16[1024,768]{0,1:T(8,128)(2,1)} %copy.11) | copy-start | bytes 4718596
  185.9 1.7 copy-start.1
Sparse Core Ops, SparseCore 0:
  87.9 24.8 reduce-scatter.1

commit v5 on v4

--- a/solution.py
+++ b/solution.py
@@ -126,7 +126,7 @@
                 self.share(source, other, self.half)
         self.second, self.third = second, third
 
-    def end(self):
+    def end(self, arrived=None):
         other = (1 - self.pool) * self.half
         for d in range(self.line):
             skip = 0 if d == 0 else self.quarter
@@ -136,11 +136,14 @@
             if d > 0:
                 self.third[d - 1].wait_recv()
                 self.share(source, other, self.quarter)
+            if d == 0:
+                self.own.wait()
+            if arrived is not None:
+                arrived((self.z + self.line - d) % self.line)
         for copy in self.kin:
             copy.wait_recv()
         for copy in self.all:
             copy.wait_send()
-        self.own.wait()
 
 
 def copy_counts(line):
@@ -154,39 +157,94 @@
     pl.semaphore_wait(barrier, len(peers))
 
 
-def gather_kernel(line, rows_ref, rows_full, own_sem, rsend, rrecv):
+def project_kernel(
+    line, scaled_ref, scale_ref, rows_ref, out_ref,
+    rows_full, kept, sent, got, own_sem, rsend, rrecv, hsend, hrecv,
+):
     def place_rows(source, begin, count):
         return rows_full.at[source, pl.ds(begin, count)]
 
+    core = lax.axis_index("tensor")
     spread = Spread(
         line, rows_ref, rows_ref.shape[0], place_rows, (rsend, rrecv), own_sem, False
     )
-    greet(spread.peers())
+    per_core = kept.shape[0]
+    tokens, width = kept.shape[1:]
+    step = 256
+
+    def head_copy(index):
+        return pltpu.make_async_remote_copy(
+            src_ref=sent.at[index],
+            dst_ref=got.at[index],
+            send_sem=hsend.at[index],
+            recv_sem=hrecv.at[index],
+            device_id=spread.sibling,
+            device_id_type=pl.DeviceIdType.MESH,
+        )
+
+    def multiply(pair, target):
+        weights = rows_full[pl.ds(pair * 2, 2)].reshape(width, -1)
+
+        def tile(index, carry):
+            rows = pl.ds(pl.multiple_of(index * step, step), step)
+            target[pair % per_core, rows] = lax.dot_general(
+                scaled_ref[rows],
+                weights,
+                (((1,), (1,)), ((), ())),
+                preferred_element_type=jnp.float32,
+            )
+            return carry
+
+        lax.fori_loop(0, tokens // step, tile, 0)
+
+    def arrived(pair):
+        @pl.when(pair // per_core == core)
+        def _():
+            multiply(pair, kept)
+
+        @pl.when(pair // per_core != core)
+        def _():
+            multiply(pair, sent)
+            head_copy(pair % per_core).start()
+
+    greet(spread.peers() + [spread.sibling])
     spread.start()
     spread.trade()
     spread.finish()
-    spread.end()
-
-
-def gather_rows(rows, group_size, collective_id):
+    spread.end(arrived)
+    for j in range(per_core):
+        head_copy(j).wait()
+        total = (kept[j] + got[j]) * scale_ref[...]
+        out_ref[:, j * width : (j + 1) * width] = total.astype(jnp.bfloat16)
+
+
+def project_rows(scaled, scale, rows, group_size, tensor_size, collective_id):
     line = group_size // 2
     few, _ = copy_counts(line)
-    any_space = pl.BlockSpec(memory_space=pl.ANY)
-    full = pl.pallas_call(
-        functools.partial(gather_kernel, line),
-        out_shape=jax.ShapeDtypeStruct((group_size,) + rows.shape, rows.dtype),
-        in_specs=[any_space],
-        out_specs=any_space,
+    tokens = scaled.shape[0]
+    per_core, width = line // tensor_size, 2 * rows.shape[0]
+    vmem = pl.BlockSpec(memory_space=pltpu.VMEM)
+    halves = pltpu.VMEM((per_core, tokens, width), jnp.float32)
+    return pl.pallas_call(
+        functools.partial(project_kernel, line),
+        out_shape=jax.ShapeDtypeStruct((tokens, per_core * width), jnp.bfloat16),
+        in_specs=[vmem, vmem, pl.BlockSpec(memory_space=pl.ANY)],
+        out_specs=vmem,
         scratch_shapes=[
+            pltpu.VMEM((group_size,) + rows.shape, rows.dtype),
+            halves,
+            halves,
+            halves,
             pltpu.SemaphoreType.DMA,
             pltpu.SemaphoreType.DMA((few,)),
             pltpu.SemaphoreType.DMA((few,)),
+            pltpu.SemaphoreType.DMA((per_core,)),
+            pltpu.SemaphoreType.DMA((per_core,)),
         ],
         compiler_params=pltpu.CompilerParams(
-            collective_id=collective_id, has_side_effects=True
+            collective_id=collective_id, has_side_effects=True, vmem_limit_bytes=48 * 2**20
         ),
-    )(rows)
-    return full.reshape((-1,) + rows.shape[1:])
+    )(scaled, scale, rows)
 
 
 def attend_one(projected, bias):
@@ -326,11 +384,17 @@
     )(slots, sources, projected, bias, cols)
 
 
-def project(hidden_in, norm_gain, rows_full, tensor_size):
+def project(hidden_in, norm_gain, w_qkv, by_kernel, group_size, tensor_size):
     slot_count, block_len, features = hidden_in.shape
     floats = hidden_in.astype(jnp.float32)
     scale = row_scale(floats, features * tensor_size).reshape(-1)
     scaled = (floats * norm_gain).astype(jnp.bfloat16).reshape(-1, features)
+    if by_kernel:
+        projected = project_rows(
+            scaled, scale[:, None], w_qkv, group_size, tensor_size, 0
+        )
+        return projected.reshape(slot_count, block_len, -1)
+    rows_full = lax.all_gather(w_qkv, "group", axis=0, tiled=True)
     contract = (((1,), (1,)), ((), ()))
     partial = lax.dot_general(
         scaled, rows_full, contract, preferred_element_type=jnp.float32
@@ -365,11 +429,9 @@
     part_rows = w_out.shape[0] // tensor_size
     own_part = lax.dynamic_slice_in_dim(w_out, own_rank * part_rows, part_rows, 0)
     by_kernel = (lax.axis_size("replica"), group_size, tensor_size) == (2, 8, 2)
-    if by_kernel:
-        rows_full = gather_rows(w_qkv, group_size, 0)
-    else:
-        rows_full = lax.all_gather(w_qkv, "group", axis=0, tiled=True)
-    projected = project(hidden_in, norm_gain, rows_full, tensor_size)
+    projected = project(
+        hidden_in, norm_gain, w_qkv, by_kernel, group_size, tensor_size
+    )
     by_head = projected.reshape(slot_count, block_len, -1, Q_PER + 2, HD)
     cache = by_head[:, :, :, Q_PER:].reshape(slot_count, block_len, -1)
     kv_cache = jnp.where(home_live[:, None, None], cache, jnp.zeros_like(cache))

time: 200 us -> 183 us (0.915)
  Pallas kernels: 136 us -> 152 us
  waiting for transfers between devices: 15.5 us -> 0 us
  between operations: 14.8 us -> 1.45 us
  matrix products: 8.64 us -> 0 us
  local copies, waits for them, and re-layouts: 12.3 us -> 15.8 us
    reduce_scatter x1 -> x0, waiting for transfers between devices: 15.5 us -> none  [project(): lax.psum_scatter(partial, 'tensor', scatter_dimension=1, tiled=True)]
    pallas_call x1, Pallas kernels: 67.9 us -> 78.1 us  [project_rows(): pl.pallas_call(functools.partial(project_kernel, line), out_shape=jax.Sha...]
    dot_general x1 -> x0, matrix products: 8.64 us -> none  [project(): lax.dot_general(scaled, rows_full, contract, preferred_element_type=jnp.f...]
    pallas_call x1, Pallas kernels: 68.2 us -> 73.9 us  [attend_and_mix(): pl.pallas_call(functools.partial(tail_kernel, line), out_shape=jax.ShapeD...]
    convert_element_type x1 -> x0, other arithmetic: 2.12 us -> none  [project(): projected = (summed * scale[:, None]).astype(jnp.bfloat16)]
    unnamed x16 -> x10, local copies, waits for them, and re-layouts: 7.46 us -> 6.73 us
  transfers between devices with their start and end apart: 1 -> 0, of which waited for: 1 -> 0; matrix products, arithmetic and copies ran while one was open for 2% -> 0% of each run, Pallas kernels for 0% -> 0%
where the time goes in v5:
time: 183 us; the launch traced here: 182 us
  Pallas kernels  152 us (83%)
  local copies, waits for them, and re-layouts  15.8 us (9%)
  other arithmetic  10.4 us (6%)
  blocking collectives  2.78 us (2%)
    pallas_call x1, Pallas kernels, project_rows(): pl.pallas_call(functools.partial(project_kernel, line), out_shape=jax.Sha...  78.1 us
    pallas_call x1, Pallas kernels, attend_and_mix(): pl.pallas_call(functools.partial(tail_kernel, line), out_shape=jax.ShapeD...  73.9 us
    unnamed x10, local copies, waits for them, and re-layouts  6.73 us
    reduce_sum x1, other arithmetic, row_scale(): partial_sq = jnp.sum(floats * floats, axis=-1)  5.32 us

profile of v5, /device:TPU:9, one launch (start us, length us, event | category | flops | bytes accessed | tf_op | source)
XLA Modules:
  0.0 182.4 jit_solution(15811568599798123409)
XLA Ops:
  0.6 0.0 copy-start
  1.4 1.2 dynamic_slice.19
  2.6 0.6 iota_compare_fusion.2
  3.3 0.8 reduce-window.9
  4.1 0.7 fusion.6
  4.8 0.6 dynamic_slice.15
  5.4 0.7 and_select_fusion.1
  6.0 0.1 select_reduce_fusion
  6.2 0.1 dynamic_slice.16.source_ref
  6.2 0.7 constant_dynamic-slice_fusion
  6.9 0.2 and_select_fusion.bias_ref
  7.2 0.0 copy-done
  7.2 0.8 constant_dynamic-slice_fusion.1.cols_ref
  8.0 5.3 %fusion.1 = (f32[8,128]{1,0:T(8,128)S(1)}, bf16[8,128,2048]{2,1,0:T(8,128)(2,1)}) fusion(bf16[8,128,2048]{2,1,0:T(8,128)(2,1)} %param.7, f32[2048]{0:T(1024)} %param.8), kind=kLoop, calls=%fused_computation.3 | loop fusion | flops 10484736 | bytes 8400896 | tf_op jit(solution)/shard_map/reduce_sum | solution.py:38
  13.3 2.8 %psum.7 = f32[8,128]{1,0:T(8,128)S(1)} all-reduce(f32[8,128]{1,0:T(8,128)S(1)} %get-tuple-element.5), channel_id=1, replica_groups=mesh['replica'=2,'group'=8,'tensor'=2] {'tensor'}, use_global_device_ids=true, to_apply=%region_3.4 | all-reduce | flops 1024 | bytes 8192 | tf_op jit(solution)/shard_map/psum | solution.py:39
  16.1 1.0 copy.12.scale_ref
  17.1 0.0 copy-start.1
  17.1 1.0 copy-done.1
  18.2 0.0 copy-start.3
  18.2 1.1 copy-done.3
  19.3 78.1 %shard_map.86 = bf16[1024,768]{1,0:T(8,128)(2,1)S(1)} custom-call(bf16[1024,2048]{1,0:T(8,128)(2,1)} %bitcast.21, f32[1024,1]{1,0:T(8,128)S(1)} %copy-done.1, bf16[192,2048]{1,0:T(8,128)(2,1)S(1)} %copy-done.3), custom_call_target="tpu_custom_call" | custom-call | tf_op jit(solution)/shard_map/pallas_call | solution.py:228
  97.4 1.6 copy.13
  99.1 1.8 %copy.15 = bf16[96,8,8,128]{3,2,1,0:T(8,128)(2,1)S(1)} copy(bf16[96,8,8,128]{3,1,2,0:T(8,128)(2,1)} %bitcast.22) | data formatting | bytes 3145728
  100.9 0.8 slice.4
  101.8 2.1 %copy.14 = bf16[8,128,256]{2,1,0:T(8,128)(2,1)} copy(bf16[8,128,256]{1,0,2:T(8,128)(2,1)} %bitcast.24) | data formatting | bytes 1048576 | tf_op jit(solution)/shard_map/reshape | solution.py:436
  103.9 1.9 %broadcast_select_fusion = bf16[8,128,256]{2,1,0:T(8,128)(2,1)} fusion(bf16[8,128,256]{2,1,0:T(8,128)(2,1)} %copy.14, pred[8]{0:T(512)(128)(4,1)S(1)} %iota_compare_fusion.2), kind=kLoop, calls=%fused_computation.4 | loop fusion | flops 262144 | bytes 1048584 | tf_op jit(solution)/shard_map/jit(_where)/select_n | solution.py:437
  105.8 0.0 copy-start.2
  105.8 1.0 copy-done.2
  106.8 73.9 %shard_map.87 = bf16[384,4096]{1,0:T(8,128)(2,1)S(1)} custom-call(s32[8]{0:T(128)S(1)} %get-tuple-element.8.slots_ref, s32[3]{0:T(128)S(1)} %dynamic_slice.16.source_ref, bf16[8,128,768]{2,1,0:T(8,128)(2,1)S(1)} %bitcast.19, f32[8,128,128]{2,1,0:T(8,128)S(1)} %and_select_fusion.bias_ref, bf16[512,512]{1,0:T(8,128)(2,1)S(1)} %copy-done.2), custom_call_target="tpu_custom_call" | custom-call | tf_op jit(solution)/shard_map/pallas_call | solution.py:366
  180.7 1.7 copy.18
  (2 shorter events, 0.0 us)
Async XLA Ops:
  0.6 6.5 %copy-start = (bf16[1024,512]{1,0:T(8,128)(2,1)S(1)}, bf16[1024,512]{1,0:T(8,128)(2,1)}, u32[]{:S(2)}) copy-start(bf16[1024,512]{1,0:T(8,128)(2,1)} %param.10) | copy-start | bytes 3145732
  17.1 1.0 copy-start.1
  18.2 1.1 copy-start.3
  105.8 1.0 copy-start.2

commit v6 on v5

--- a/solution.py
+++ b/solution.py
@@ -158,8 +158,9 @@
 
 
 def project_kernel(
-    line, scaled_ref, scale_ref, rows_ref, out_ref,
-    rows_full, kept, sent, got, own_sem, rsend, rrecv, hsend, hrecv,
+    line, model_width, hidden_ref, gain_ref, rows_ref, out_ref,
+    rows_full, kept, sent, got, scaled_ref, squares, own_sem, rsend, rrecv, hsend, hrecv,
+    qsend, qrecv,
 ):
     def place_rows(source, begin, count):
         return rows_full.at[source, pl.ds(begin, count)]
@@ -207,26 +208,46 @@
             multiply(pair, sent)
             head_copy(pair % per_core).start()
 
+    def prepare(index, carry):
+        rows = pl.ds(pl.multiple_of(index * 64, 64), 64)
+        floats = hidden_ref[rows].astype(jnp.float32)
+        scaled_ref[rows] = (floats * gain_ref[...]).astype(jnp.bfloat16)
+        partial_sq = jnp.sum(floats * floats, axis=-1, keepdims=True)
+        squares[0, rows] = jnp.broadcast_to(partial_sq, (64, squares.shape[2]))
+        return carry
+
     greet(spread.peers() + [spread.sibling])
     spread.start()
+    lax.fori_loop(0, tokens // 64, prepare, 0)
+    square_copy = pltpu.make_async_remote_copy(
+        src_ref=squares.at[0],
+        dst_ref=squares.at[1],
+        send_sem=qsend,
+        recv_sem=qrecv,
+        device_id=spread.sibling,
+        device_id_type=pl.DeviceIdType.MESH,
+    )
+    square_copy.start()
     spread.trade()
     spread.finish()
     spread.end(arrived)
+    square_copy.wait()
+    scale = lax.rsqrt((squares[0, :, :1] + squares[1, :, :1]) / model_width + epsilon)
     for j in range(per_core):
         head_copy(j).wait()
-        total = (kept[j] + got[j]) * scale_ref[...]
+        total = (kept[j] + got[j]) * scale
         out_ref[:, j * width : (j + 1) * width] = total.astype(jnp.bfloat16)
 
 
-def project_rows(scaled, scale, rows, group_size, tensor_size, collective_id):
+def project_rows(hidden, gain, rows, group_size, tensor_size, collective_id):
     line = group_size // 2
     few, _ = copy_counts(line)
-    tokens = scaled.shape[0]
+    tokens, features = hidden.shape
     per_core, width = line // tensor_size, 2 * rows.shape[0]
     vmem = pl.BlockSpec(memory_space=pltpu.VMEM)
     halves = pltpu.VMEM((per_core, tokens, width), jnp.float32)
     return pl.pallas_call(
-        functools.partial(project_kernel, line),
+        functools.partial(project_kernel, line, features * tensor_size),
         out_shape=jax.ShapeDtypeStruct((tokens, per_core * width), jnp.bfloat16),
         in_specs=[vmem, vmem, pl.BlockSpec(memory_space=pl.ANY)],
         out_specs=vmem,
@@ -235,16 +256,20 @@
             halves,
             halves,
             halves,
+            pltpu.VMEM((tokens, features), jnp.bfloat16),
+            pltpu.VMEM((2, tokens, HD), jnp.float32),
             pltpu.SemaphoreType.DMA,
             pltpu.SemaphoreType.DMA((few,)),
             pltpu.SemaphoreType.DMA((few,)),
             pltpu.SemaphoreType.DMA((per_core,)),
             pltpu.SemaphoreType.DMA((per_core,)),
+            pltpu.SemaphoreType.DMA,
+            pltpu.SemaphoreType.DMA,
         ],
         compiler_params=pltpu.CompilerParams(
             collective_id=collective_id, has_side_effects=True, vmem_limit_bytes=48 * 2**20
         ),
-    )(scaled, scale, rows)
+    )(hidden, gain, rows)
 
 
 def attend_one(projected, bias):
@@ -386,14 +411,15 @@
 
 def project(hidden_in, norm_gain, w_qkv, by_kernel, group_size, tensor_size):
     slot_count, block_len, features = hidden_in.shape
+    if by_kernel:
+        flat = hidden_in.reshape(-1, features)
+        projected = project_rows(
+            flat, norm_gain[None], w_qkv, group_size, tensor_size, 0
+        )
+        return projected.reshape(slot_count, block_len, -1)
     floats = hidden_in.astype(jnp.float32)
     scale = row_scale(floats, features * tensor_size).reshape(-1)
     scaled = (floats * norm_gain).astype(jnp.bfloat16).reshape(-1, features)
-    if by_kernel:
-        projected = project_rows(
-            scaled, scale[:, None], w_qkv, group_size, tensor_size, 0
-        )
-        return projected.reshape(slot_count, block_len, -1)
     rows_full = lax.all_gather(w_qkv, "group", axis=0, tiled=True)
     contract = (((1,), (1,)), ((), ()))
     partial = lax.dot_general(

time: 183 us -> 173 us (0.945)
  other arithmetic: 10.4 us -> 5.08 us
  blocking collectives: 2.78 us -> 0 us
    reduce_sum x1 -> x0, other arithmetic: 5.32 us -> none  [row_scale(): partial_sq = jnp.sum(floats * floats, axis=-1)]
    psum x1 -> x0, blocking collectives: 2.78 us -> none  [row_scale(): summed = lax.psum(partial_sq, 'tensor')]
where the time goes in v6:
time: 173 us; the launch traced here: 172 us
  Pallas kernels  151 us (87%)
  local copies, waits for them, and re-layouts  14.4 us (8%)
  other arithmetic  5.08 us (3%)
    pallas_call x1, Pallas kernels, project_rows(): pl.pallas_call(functools.partial(project_kernel, line, features * tensor_...  78.1 us
    pallas_call x1, Pallas kernels, attend_and_mix(): pl.pallas_call(functools.partial(tail_kernel, line), out_shape=jax.ShapeD...  73.1 us
    unnamed x10, local copies, waits for them, and re-layouts  6.39 us

profile of v6, /device:TPU:9, one launch (start us, length us, event | category | flops | bytes accessed | tf_op | source)
XLA Modules:
  0.0 172.1 jit_solution(14751216671130647298)
XLA Ops:
  0.6 0.0 copy-start
  1.4 1.2 dynamic_slice.19
  2.6 0.6 iota_compare_fusion.2
  3.3 0.8 reduce-window.9
  4.1 0.7 fusion.4
  4.8 0.6 dynamic_slice.15
  5.4 0.7 and_select_fusion.1
  6.0 0.1 select_reduce_fusion
  6.2 0.1 dynamic_slice.16.source_ref
  6.2 0.7 constant_dynamic-slice_fusion
  6.9 0.2 and_select_fusion.bias_ref
  7.2 0.0 copy-done
  7.2 0.8 constant_dynamic-slice_fusion.1.cols_ref
  8.0 0.0 copy-start.2
  8.0 1.1 copy-done.2
  9.1 0.0 copy-start.3
  9.1 0.7 copy-done.3
  9.8 78.1 %shard_map.86 = bf16[1024,768]{1,0:T(8,128)(2,1)S(1)} custom-call(bf16[1024,2048]{1,0:T(8,128)(2,1)} %bitcast.23, f32[1,2048]{1,0:T(1,128)S(1)} %bitcast.21, bf16[192,2048]{1,0:T(8,128)(2,1)S(1)} %copy-done.2), custom_call_target="tpu_custom_call" | custom-call | tf_op jit(solution)/shard_map/pallas_call | solution.py:249
  87.9 1.6 copy.11
  89.6 1.8 %copy.13 = bf16[96,8,8,128]{3,2,1,0:T(8,128)(2,1)S(1)} copy(bf16[96,8,8,128]{3,1,2,0:T(8,128)(2,1)} %bitcast.22) | data formatting | bytes 3145728
  91.4 0.8 slice.4
  92.2 2.1 %copy.12 = bf16[8,128,256]{2,1,0:T(8,128)(2,1)} copy(bf16[8,128,256]{1,0,2:T(8,128)(2,1)} %bitcast.25) | data formatting | bytes 1048576 | tf_op jit(solution)/shard_map/reshape | solution.py:462
  94.4 1.9 %broadcast_select_fusion = bf16[8,128,256]{2,1,0:T(8,128)(2,1)} fusion(bf16[8,128,256]{2,1,0:T(8,128)(2,1)} %copy.12, pred[8]{0:T(512)(128)(4,1)S(1)} %iota_compare_fusion.2), kind=kLoop, calls=%fused_computation | loop fusion | flops 262144 | bytes 1048584 | tf_op jit(solution)/shard_map/jit(_where)/select_n | solution.py:463
  96.3 0.0 copy-start.1
  96.3 1.0 copy-done.1
  97.3 73.1 %shard_map.87 = bf16[384,4096]{1,0:T(8,128)(2,1)S(1)} custom-call(s32[8]{0:T(128)S(1)} %get-tuple-element.6.slots_ref, s32[3]{0:T(128)S(1)} %dynamic_slice.16.source_ref, bf16[8,128,768]{2,1,0:T(8,128)(2,1)S(1)} %bitcast.19, f32[8,128,128]{2,1,0:T(8,128)S(1)} %and_select_fusion.bias_ref, bf16[512,512]{1,0:T(8,128)(2,1)S(1)} %copy-done.1), custom_call_target="tpu_custom_call" | custom-call | tf_op jit(solution)/shard_map/pallas_call | solution.py:391
  170.5 1.7 copy.16
  (1 shorter events, 0.0 us)
Async XLA Ops:
  0.6 6.5 %copy-start = (bf16[1024,512]{1,0:T(8,128)(2,1)S(1)}, bf16[1024,512]{1,0:T(8,128)(2,1)}, u32[]{:S(2)}) copy-start(bf16[1024,512]{1,0:T(8,128)(2,1)} %param.10) | copy-start | bytes 3145732
  8.0 1.1 copy-start.2
  9.1 0.7 copy-start.3
  96.3 1.0 copy-start.1

commit v7 on v6

--- a/solution.py
+++ b/solution.py
@@ -459,7 +459,10 @@
         hidden_in, norm_gain, w_qkv, by_kernel, group_size, tensor_size
     )
     by_head = projected.reshape(slot_count, block_len, -1, Q_PER + 2, HD)
-    cache = by_head[:, :, :, Q_PER:].reshape(slot_count, block_len, -1)
+    if projected.shape[-1] == (Q_PER + 2) * HD:
+        cache = projected[:, :, Q_PER * HD :]
+    else:
+        cache = by_head[:, :, :, Q_PER:].reshape(slot_count, block_len, -1)
     kv_cache = jnp.where(home_live[:, None, None], cache, jnp.zeros_like(cache))
     slots = jnp.minimum(send_slot, slot_count - 1)
     if by_kernel:

time: 173 us -> 163 us (0.942)
  local copies, waits for them, and re-layouts: 14.4 us -> 6.14 us
    unnamed x10 -> x7, local copies, waits for them, and re-layouts: 6.39 us -> 3.5 us
    reshape x1 -> x0, local copies, waits for them, and re-layouts: 2.11 us -> none  [per_device(): cache = by_head[:, :, :, Q_PER:].reshape(slot_count, block_len, -1)]
where the time goes in v7:
time: 163 us
  Pallas kernels  151 us (93%)
  local copies, waits for them, and re-layouts  6.14 us (4%)
  other arithmetic  4.04 us (2%)
    pallas_call x1, Pallas kernels, project_rows(): pl.pallas_call(functools.partial(project_kernel, line, features * tensor_...  78.1 us
    pallas_call x1, Pallas kernels, attend_and_mix(): pl.pallas_call(functools.partial(tail_kernel, line), out_shape=jax.ShapeD...  73.1 us
    unnamed x7, local copies, waits for them, and re-layouts  3.5 us

profile of v7, /device:TPU:9, one launch (start us, length us, event | category | flops | bytes accessed | tf_op | source)
XLA Modules:
  0.0 162.8 jit_solution(13828670308504324655)
XLA Ops:
  0.6 0.0 copy-start
  1.4 1.2 dynamic_slice.19
  2.6 0.6 iota_compare_fusion.2
  3.3 0.8 reduce-window.9
  4.1 0.7 fusion.4
  4.8 0.6 dynamic_slice.15
  5.4 0.7 and_select_fusion.1
  6.0 0.1 select_reduce_fusion
  6.2 0.1 dynamic_slice.16.source_ref
  6.2 0.7 constant_dynamic-slice_fusion
  6.9 0.2 and_select_fusion.bias_ref
  7.2 0.0 copy-done
  7.2 0.0 copy-start.1
  7.2 1.1 copy-done.1
  8.4 0.0 copy-start.2
  8.4 0.7 copy-done.2
  9.0 78.1 %shard_map.86 = bf16[1024,768]{1,0:T(8,128)(2,1)S(1)} custom-call(bf16[1024,2048]{1,0:T(8,128)(2,1)} %bitcast.17, f32[1,2048]{1,0:T(1,128)S(1)} %bitcast.16, bf16[192,2048]{1,0:T(8,128)(2,1)S(1)} %copy-done.1), custom_call_target="tpu_custom_call" | custom-call | tf_op jit(solution)/shard_map/pallas_call | solution.py:249
  87.2 0.9 slice_select_fusion
  88.1 73.1 %shard_map.87 = bf16[384,4096]{1,0:T(8,128)(2,1)S(1)} custom-call(s32[8]{0:T(128)S(1)} %get-tuple-element.6.slots_ref, s32[3]{0:T(128)S(1)} %dynamic_slice.16.source_ref, bf16[8,128,768]{2,1,0:T(8,128)(2,1)S(1)} %bitcast.15, f32[8,128,128]{2,1,0:T(8,128)S(1)} %and_select_fusion.bias_ref, bf16[512,512]{1,0:T(8,128)(2,1)S(1)} %constant_dynamic-slice_fusion.1.cols_ref), custom_call_target="tpu_custom_call" | custom-call | tf_op jit(solution)/shard_map/pallas_call | solution.py:391
  161.2 1.7 %copy.11 = bf16[3,128,4096]{2,1,0:T(8,128)(2,1)} copy(bf16[3,128,4096]{2,1,0:T(8,128)(2,1)S(1)} %bitcast.13) | data formatting | bytes 6291456
  (2 shorter events, 0.1 us)
Async XLA Ops:
  0.6 6.5 %copy-start = (bf16[1024,512]{1,0:T(8,128)(2,1)S(1)}, bf16[1024,512]{1,0:T(8,128)(2,1)}, u32[]{:S(2)}) copy-start(bf16[1024,512]{1,0:T(8,128)(2,1)} %param.10) | copy-start | bytes 3145732
  7.2 1.1 copy-start.1
  8.4 0.7 copy-start.2
